TPU v7x, 1024 devices: a whole 4x8x16 slice. The times are simulated.
1024 devices in a mesh: expert: 64 (over z, x), dp: 16 (over y, core).
Axes of the slice: x: 4, y: 8, z: 16, core: 2. Of those that a mesh axis runs over, the one named last changes fastest.
Arguments:
- cotangent: bfloat16 [16, 12288, 1024], P('dp', 'expert'), may hold values from -4 to 4
- route_weights: float32 [16, 12288, 8], P('dp', 'expert'), may hold values from 0.02 to 0.5
- expert_ids: int32 [16, 12288, 8], P('dp', 'expert'), may hold values from 0 to 63, as said below
- slot_index: int32 [16, 12288, 8], P('dp', 'expert'), may hold values from 0 to 23, as said below
- hidden: bfloat16 [16, 64, 1536, 384], P('dp', 'expert'), may hold values from -6 to 6
- carried_error: bfloat16 [16, 64, 384, 1024], P('dp', 'expert'), may hold values from -6 to 6
- q_factor: float32 [64, 16, 1024], P('expert'), may hold values from -0.1875 to 0.1875
Outputs:
- new_error: bfloat16 [16, 64, 384, 1024], P('dp', 'expert')
- q_next: float32 [64, 16, 1024], P('expert')
Inputs may be any that keep to these rules, and one draw needn't show every extreme that they name: `expert_ids`: each token names 8 different experts. The tokens of one device name one expert at most 24 times, and in each replica one expert is named exactly 24 times by the tokens of every device of that replica. `slot_index`: among the tokens of one device, the routes to one expert carry different slots.
All inputs are finite; a program needn't handle non-finite values.
Results may differ from a plain program's by a relative error of at most 0.017.
Values may be sent and summed in bfloat16 or wider, within the bound.
A program may use at most 32 MiB of HBM per device.

v0:
```python
import jax
import jax.numpy as jnp
from jax import lax
from jax.sharding import PartitionSpec as P

highest = lax.Precision.HIGHEST


def orthonormal(factor_rows):
    gram_matrix = jnp.dot(factor_rows, factor_rows.T, precision=highest)
    lower_factor = jnp.linalg.cholesky(gram_matrix)
    return lax.linalg.triangular_solve(lower_factor, factor_rows, left_side=True, lower=True)


def shards(cotangent, route_weights, expert_ids, slot_index, hidden, carried_error, q_factor):
    peer_count = lax.axis_size("expert")
    replicas = lax.axis_size("dp")
    tokens = cotangent[0]
    model_dim = tokens.shape[1]
    expert_rows = hidden[0, 0]
    capacity = expert_rows.shape[0]
    per_source = capacity // peer_count
    scaled = (route_weights[0][:, :, None] * tokens[:, None, :].astype(jnp.float32)).astype(
        jnp.bfloat16
    )
    target = (expert_ids[0] * per_source + slot_index[0]).reshape(-1)
    outgoing = (
        jnp.zeros((capacity, model_dim), jnp.bfloat16)
        .at[target]
        .set(scaled.reshape(-1, model_dim), unique_indices=True)
    )
    outgoing = outgoing.reshape(peer_count, per_source, model_dim)
    error_full = carried_error[0, 0].astype(jnp.float32)
    q_rows = q_factor[0]
    arrived = lax.all_to_all(outgoing, "expert", split_axis=0, concat_axis=0, tiled=True)
    flattened = arrived.reshape(capacity, arrived.shape[2])
    gradient = lax.dot_general(
        expert_rows, flattened, (((0,), (0,)), ((), ())), preferred_element_type=jnp.float32
    )
    merged = gradient + error_full
    left_local = jnp.dot(q_rows, merged.T, precision=highest)
    left_sum = lax.psum(left_local, "dp") / replicas
    basis_rows = orthonormal(left_sum)
    q_local = jnp.dot(basis_rows, merged, precision=highest)
    q_next = lax.psum(q_local.astype(jnp.bfloat16), "dp").astype(jnp.float32) / replicas
    new_error = (merged - jnp.dot(basis_rows.T, q_next, precision=highest)).astype(jnp.bfloat16)
    return (new_error[None, None], q_next[None])


def solution(mesh):
    return jax.shard_map(
        shards,
        mesh=mesh,
        in_specs=(
            P("dp", "expert", None),
            P("dp", "expert", None),
            P("dp", "expert", None),
            P("dp", "expert", None),
            P("dp", "expert", None, None),
            P("dp", "expert", None, None),
            P("expert", None, None),
        ),
        out_specs=(P("dp", "expert", None, None), P("expert", None, None)),
        check_vma=False,
    )
```

profile of v0, /device:TPU:1, one launch (start us, length us, event | category | flops | bytes accessed | tf_op | source)
XLA Modules:
  0.0 287.6 jit_solution(8521303970375798693)
XLA Ops:
  0.6 0.0 copy-start
  0.6 1.2 bitcast_convert_fusion
  1.8 0.7 multiply_add_fusion
  2.5 0.1 copy.13
  2.7 0.1 add.46
  2.8 0.8 copy.14
  3.6 0.1 mul.35
  3.7 10.3 %scatter_custom_fusion = bf16[1536,1024]{1,0:T(8,128)(2,1)} fusion(s32[1536]{0:T(1024)S(1)} %fusion.20, f32[192,1024]{1,0:T(8,128)S(1)} %bitcast_convert_fusion, f32[1536]{0:T(1024)S(1)} %mul.35, bf16[]{:T(256)} %constant.45.clone.1), kind=kCustom, calls=%fused_computation.3 | custom fusion | flops 3145728 | bytes 3940354 | tf_op jit(solution)/shard_map/scatter | solution.py:30
  14.0 0.0 copy-start.1
  14.0 23.1 %all-to-all-start = ((bf16[64,24,1024]{2,1,0:T(8,128)(2,1)}), bf16[64,24,1024]{2,1,0:T(8,128)(2,1)}, u32[]{:S(2)}, u32[]{:S(2)}) async-start(bf16[64,24,1024]{2,1,0:T(8,128)(2,1)} %bitcast.41), calls=%async_computation | async-start | bytes 6291456 | tf_op jit(solution)/shard_map/all_to_all | solution.py:35
  37.1 0.0 copy-done.1
  37.1 0.4 copy.15
  37.5 139.7 %all-to-all-done = bf16[64,24,1024]{2,1,0:T(8,128)(2,1)} async-done(((bf16[64,24,1024]{2,1,0:T(8,128)(2,1)}), bf16[64,24,1024]{2,1,0:T(8,128)(2,1)}, u32[]{:S(2)}, u32[]{:S(2)}) %all-to-all-start) | async-done | bytes 3145760 | tf_op jit(solution)/shard_map/all_to_all | solution.py:35
  177.2 0.0 copy-done
  177.2 0.0 copy-start.3
  177.2 3.8 %convert_add_fusion = f32[384,1024]{0,1:T(8,128)S(1)} fusion(bf16[1536,1024]{1,0:T(8,128)(2,1)} %bitcast.3, bf16[1,1,1536,384]{3,2,1,0:T(8,128)(2,1)S(1)} %copy-done, bf16[1,1,384,1024]{2,3,1,0:T(8,128)(2,1)S(1)} %copy.15), kind=kOutput, calls=%fused_computation.6 | convolution fusion | flops 1208745984 | bytes 6684672 | tf_op jit(solution)/shard_map/dot_general | solution.py:37
  181.0 0.0 copy-done.3
  181.0 0.9 convolution_bitcast_fusion
  181.9 48.6 %psum.14 = f32[16,384]{1,0:T(8,128)S(1)} all-reduce(f32[16,384]{1,0:T(8,128)S(1)} %convolution_bitcast_fusion), channel_id=1, replica_groups=mesh['expert'=64,'dp'=16] {'dp'}, use_global_device_ids=true, to_apply=%region_1.0 | all-reduce | flops 6144 | bytes 49152 | tf_op jit(solution)/shard_map/psum | solution.py:42
  230.5 0.1 fusion.13
  230.7 0.1 copy.16
  230.8 1.5 cholesky.16
  232.3 0.6 compare_reduce_fusion
  232.9 0.6 fusion.17
  233.6 1.2 custom-call.6
  234.8 0.2 fusion.11
  235.0 0.0 copy-start.2
  235.1 0.6 copy-done.2
  235.7 1.4 convolution_convert_fusion
  237.1 45.7 %psum.15 = bf16[16,1024]{1,0:T(8,128)(2,1)} all-reduce(bf16[16,1024]{1,0:T(8,128)(2,1)S(1)} %convolution_convert_fusion), channel_id=1, replica_groups=mesh['expert'=64,'dp'=16] {'dp'}, use_global_device_ids=true, to_apply=%region_4.5 | all-reduce | flops 16384 | bytes 65536 | tf_op jit(solution)/shard_map/psum | solution.py:45
  282.8 2.2 fusion.6
  285.0 1.4 fusion.9
  286.4 1.2 copy.18
  (3 shorter events, 0.1 us)
Async XLA Ops:
  0.6 176.6 %copy-start = (bf16[1,1,1536,384]{3,2,1,0:T(8,128)(2,1)S(1)}, bf16[1,1,1536,384]{3,2,1,0:T(8,128)(2,1)}, u32[]{:S(2)}) copy-start(bf16[1,1,1536,384]{3,2,1,0:T(8,128)(2,1)} %param.11) | copy-start | bytes 3538948
  14.0 23.2 %copy-start.1 = (bf16[1,1,384,1024]{3,2,1,0:T(8,128)(2,1)S(1)}, bf16[1,1,384,1024]{3,2,1,0:T(8,128)(2,1)}, u32[]{:S(2)}) copy-start(bf16[1,1,384,1024]{3,2,1,0:T(8,128)(2,1)} %param.12) | copy-start | bytes 2359300
  14.0 163.2 %all-to-all-start = ((bf16[64,24,1024]{2,1,0:T(8,128)(2,1)}), bf16[64,24,1024]{2,1,0:T(8,128)(2,1)}, u32[]{:S(2)}, u32[]{:S(2)}) async-start(bf16[64,24,1024]{2,1,0:T(8,128)(2,1)} %bitcast.41), calls=%async_computation | async-start | bytes 6291456 | tf_op jit(solution)/shard_map/all_to_all | solution.py:35
  177.2 3.8 %copy-start.3 = (f32[1,16,1024]{2,1,0:T(8,128)S(1)}, f32[1,16,1024]{2,1,0:T(8,128)}, u32[]{:S(2)}) copy-start(f32[1,16,1024]{2,1,0:T(8,128)} %param.13) | copy-start | bytes 196612
  235.0 0.6 copy-start.2
where the time goes:
time: 291 us; the launch traced here: 288 us
  waiting for transfers between devices  140 us (48%)
  blocking collectives  94.4 us (32%)
  starting transfers between devices  23.1 us (8%)
  other arithmetic  17.6 us (6%)
  matrix products  8.71 us (3%)
  local copies, waits for them, and re-layouts  3.34 us (1%)
    all_to_all x1, waiting for transfers between devices, shards(): lax.all_to_all(outgoing, 'expert', split_axis=0, concat_axis=0, tiled=True)  140 us
    psum x1, blocking collectives, shards(): left_sum = lax.psum(left_local, 'dp') / replicas  48.6 us
    psum x1, blocking collectives, shards(): lax.psum(q_local.astype(jnp.bfloat16), 'dp').astype(jnp.float32) / replicas  45.7 us
    all_to_all x1, starting transfers between devices, shards(): lax.all_to_all(outgoing, 'expert', split_axis=0, concat_axis=0, tiled=True)  23.1 us
    scatter x1, other arithmetic, shards(): outgoing = jnp.zeros((capacity, model_dim), jnp.bfloat16).at[target].set(...  10.3 us
  transfers between devices with their start and end apart: 1, of which 1 were waited for; matrix products, arithmetic and copies ran while one was open for 0% of the time, Pallas kernels for 0%

commit v1 on v0

v1 whole, which is shorter than its diff:
```python
import functools

import jax
import jax.numpy as jnp
from jax import lax
from jax.experimental import pallas as pl
from jax.experimental.pallas import tpu as pltpu
from jax.sharding import PartitionSpec as P

highest = lax.Precision.HIGHEST
MESH = pl.DeviceIdType.MESH
f32 = jnp.float32
bf16 = jnp.bfloat16

X_CHIPS = 4
PARTS = 4
PAD = 32


def thirds(value):
    first = value.astype(bf16).astype(f32)
    second = (value - first).astype(bf16).astype(f32)
    return first, second, value - first - second


def route_kernel(
    nz, nx, send,
    cot, weights, ids, slots, hidden_hbm, error_hbm, merged,
    ring, meta, own_meta, picked, arrived, picked_own, arrived_own, picked_far, arrived_far,
    hidden, error,
    local_sem, ring_send, ring_recv, meta_send, meta_recv, x_send, x_recv,
):
    half = nz // 2
    tokens, model_dim = cot.shape
    width = model_dim // PARTS
    lanes = nx * send
    me = lax.axis_index("expert")
    z = lax.div(me, nx)
    x = lax.rem(me, nx)
    right = lax.rem(z + 1, nz) * nx + x
    left = lax.rem(z + nz - 1, nz) * nx + x
    sides = (right, left)

    load_hidden = pltpu.make_async_copy(hidden_hbm, hidden, local_sem.at[0])
    load_error = pltpu.make_async_copy(error_hbm, error, local_sem.at[1])
    load_hidden.start()
    load_error.start()

    barrier = pltpu.get_barrier_semaphore()
    partners = [right, left] + [z * nx + lax.rem(x + step, nx) for step in range(1, nx)]
    for partner in partners:
        pl.semaphore_signal(barrier, inc=1, device_id={"expert": partner}, device_id_type=MESH)
    pl.semaphore_wait(barrier, len(partners))

    def ring_copy(side, hop, part, source=None):
        return pltpu.make_async_remote_copy(
            src_ref=ring.at[side, hop - 2, part] if source is None else source,
            dst_ref=ring.at[side, hop - 1, part],
            send_sem=ring_send.at[side, hop - 1, part],
            recv_sem=ring_recv.at[side, hop - 1, part],
            device_id={"expert": sides[side]},
            device_id_type=MESH,
        )

    def own_copy(side, part):
        return ring_copy(side, 1, part, cot.at[:, pl.ds(part * width, width)])

    def meta_copy(side, hop):
        return pltpu.make_async_remote_copy(
            src_ref=meta.at[side, hop - 1],
            dst_ref=meta.at[side, hop],
            send_sem=meta_send.at[side, hop - 1],
            recv_sem=meta_recv.at[side, hop - 1],
            device_id={"expert": sides[side]},
            device_id_type=MESH,
        )

    def x_copy(pick, land, group, part, step, source=None):
        target = lax.rem(x + step, nx)
        source = x if source is None else source
        return pltpu.make_async_remote_copy(
            src_ref=pick.at[part, target],
            dst_ref=land.at[part, source],
            send_sem=x_send.at[group, part, step - 1],
            recv_sem=x_recv.at[group, part, step - 1],
            device_id={"expert": z * nx + target},
            device_id_type=MESH,
        )

    for part in range(PARTS):
        for side in range(2):
            own_copy(side, part).start()

    lane = lax.broadcasted_iota(jnp.int32, (tokens, 128), 1)
    token = lax.broadcasted_iota(jnp.int32, (tokens, 128), 0).astype(f32)
    level = lax.div(ids[...], nx)
    place = lax.rem(ids[...], nx) * send + slots[...]
    to_right = lax.rem(level - z - 1 + 2 * nz, nz)
    to_left = lax.rem(z - level - 1 + 2 * nz, nz)
    table = jnp.zeros((128, 512), f32)
    for k in range(ids.shape[1]):
        row = (lane == to_right[:, k : k + 1]) | (lane == 16 + to_left[:, k : k + 1])
        hit = lane == place[:, k : k + 1]
        values = [token] + list(thirds(jnp.broadcast_to(weights[:, k : k + 1], (tokens, 128))))
        values = jnp.concatenate([jnp.where(hit, v, 0.0) for v in values], axis=1).astype(bf16)
        table += lax.dot_general(
            jnp.where(row, 1.0, 0.0).astype(bf16), values, (((0,), (0,)), ((), ())),
            preferred_element_type=f32,
        )
    which = table[:, :128]
    gain = (table[:, 384:] + table[:, 256:384]) + table[:, 128:256]
    for side in range(2):
        meta[side, 0, 0:8, :] = which[16 * side : 16 * side + 8]
        meta[side, 0, 8:16, :] = gain[16 * side : 16 * side + 8]
        meta_copy(side, 1).start()
    own_meta[0:16, :] = which[0:16]
    own_meta[16:32, :] = gain[0:16]

    token_lane = lax.broadcasted_iota(jnp.int32, (lanes, tokens), 1).astype(f32)

    def columns(rows):
        stacked = jnp.concatenate(rows + [jnp.zeros((8 - len(rows), 128), f32)], axis=0)
        turned = jnp.transpose(stacked)[:lanes]
        return [turned[:, i : i + 1] for i in range(len(rows))]

    def one_hot(which_column):
        return jnp.where(token_lane == which_column, 1.0, 0.0).astype(bf16)

    def pick_rows(blocks, pick, land, group, part, rows):
        chosen = [
            jnp.dot(choice, block, preferred_element_type=f32) * scale
            for choice, scale, block in blocks
        ]
        pad = rows - send * len(blocks)
        filler = [jnp.zeros((pad, width), f32)] if pad else []
        for target in range(nx):
            cut = [c[target * send : (target + 1) * send] for c in chosen]
            pick[part, target] = jnp.concatenate(cut + filler, axis=0).astype(bf16)
        for step in range(1, nx):
            x_copy(pick, land, group, part, step).start()
        land[part, x] = pick[part, x]

    def hidden_rows(levels, rows):
        blocks = [hidden[v].astype(f32) for v in levels]
        pad = rows - send * len(levels)
        filler = [jnp.zeros((pad, hidden.shape[2]), f32)] if pad else []
        pieces = []
        for source in range(nx):
            pieces += [b[source * send : (source + 1) * send] for b in blocks] + filler
        return jnp.transpose(jnp.concatenate(pieces, axis=0)).astype(bf16)

    def accumulate(land, pick, group, levels, rows, order=range(PARTS)):
        turned = hidden_rows(levels, rows)
        for part in order:
            for step in range(1, nx):
                x_copy(pick, land, group, part, step, lax.rem(x + nx - step, nx)).wait_recv()
            block = land[part].reshape(nx * rows, width)
            merged[:, pl.ds(part * width, width)] += jnp.dot(
                turned, block, preferred_element_type=f32
            )

    def pair_levels(hop):
        return [lax.rem(z - hop + nz, nz), lax.rem(z + hop, nz)]

    def step_hop(hop, forward):
        choices = None
        for part in range(PARTS):
            for side in range(2):
                ring_copy(side, hop, part, cot.at[:, pl.ds(0, width)]).wait_recv()
                if forward(side, part):
                    ring_copy(side, hop + 1, part).start()
            if choices is None:
                for side in range(2):
                    meta_copy(side, hop).wait_recv()
                    if forward(side, None):
                        meta_copy(side, hop + 1).start()
                got = columns(
                    [meta[s, hop, pl.ds(hop - 1, 1), :] for s in range(2)]
                    + [meta[s, hop, pl.ds(hop + 7, 1), :] for s in range(2)]
                )
                choices = [(one_hot(got[s]), got[2 + s]) for s in range(2)]
            blocks = [choices[s] + (ring[s, hop - 1, part],) for s in range(2)]
            pick_rows(blocks, picked.at[hop - 1], arrived.at[hop - 1], hop - 1, part, 2 * send)

    def add_hop(hop):
        accumulate(arrived.at[hop - 1], picked.at[hop - 1], hop - 1, pair_levels(hop), 2 * send)

    got = columns([own_meta[nz - 1 : nz, :], own_meta[nz + 15 : nz + 16, :]])
    own_choice = (one_hot(got[0]), got[1])
    for part in range(PARTS):
        block = cot[:, part * width : (part + 1) * width]
        pick_rows([own_choice + (block,)], picked_own, arrived_own, half - 1, part, PAD)
    load_error.wait()
    merged[...] = error[...].astype(f32)
    load_hidden.wait()

    everything = lambda side, part: True
    last = lambda side, part: (side == 0) if part is None else (part < PARTS // 2) == (side == 0)
    step_hop(1, everything)
    accumulate(arrived_own, picked_own, half - 1, [z], PAD)

    def body(hop, carry):
        step_hop(hop, everything)
        add_hop(hop - 1)
        return carry

    lax.fori_loop(2, half - 1, body, 0)
    step_hop(half - 1, last)
    add_hop(half - 2)

    meta_copy(0, half).wait_recv()
    got = columns([meta[0, half, half - 1 : half, :], meta[0, half, half + 7 : half + 8, :]])
    far_choice = (one_hot(got[0]), got[1])
    order = []
    for part in range(PARTS // 2):
        order += [(0, part), (1, part + PARTS // 2)]
    for side, part in order:
        ring_copy(side, half, part, cot.at[:, pl.ds(0, width)]).wait_recv()
        block = ring[side, half - 1, part]
        pick_rows([far_choice + (block,)], picked_far, arrived_far, half, part, PAD)
    add_hop(half - 1)
    far = lax.rem(z + half, nz)
    accumulate(arrived_far, picked_far, half, [far], PAD, [part for _, part in order])

    for part in range(PARTS):
        for side in range(2):
            own_copy(side, part).wait_send()
    for side in range(2):
        meta_copy(side, 1).wait_send()

    def drain(hop, carry):
        for part in range(PARTS):
            for side in range(2):
                ring_copy(side, hop, part).wait_send()
        for side in range(2):
            meta_copy(side, hop).wait_send()
        return carry

    lax.fori_loop(2, half, drain, 0)
    for side, part in order:
        ring_copy(side, half, part).wait_send()
    meta_copy(0, half).wait_send()

    def drain_x(group, carry):
        for part in range(PARTS):
            for step in range(1, nx):
                x_copy(picked.at[group], arrived.at[group], group, part, step).wait_send()
        return carry

    lax.fori_loop(0, half - 1, drain_x, 0)
    for pick, land, group in (
        (picked_own, arrived_own, half - 1),
        (picked_far, arrived_far, half),
    ):
        for part in range(PARTS):
            for step in range(1, nx):
                x_copy(pick, land, group, part, step).wait_send()


def factor_kernel(
    replicas,
    merged, q_rows, new_error, q_next,
    left_out, left_in, left_all, right_out, right_in, right_all, send_sem, recv_sem,
):
    me = lax.axis_index("dp")
    rank = q_rows.shape[0]

    if replicas > 1:
        barrier = pltpu.get_barrier_semaphore()
        for step in range(1, replicas):
            pl.semaphore_signal(
                barrier, inc=1, device_id={"dp": lax.rem(me + step, replicas)}, device_id_type=MESH
            )
        pl.semaphore_wait(barrier, replicas - 1)

    share = rank // replicas

    def copy(source, target, stage, step, origin):
        return pltpu.make_async_remote_copy(
            src_ref=source,
            dst_ref=target.at[origin],
            send_sem=send_sem.at[stage, step - 1],
            recv_sem=recv_sem.at[stage, step - 1],
            device_id={"dp": lax.rem(me + step, replicas)},
            device_id_type=MESH,
        )

    def begin_sum(value, out, into, stage):
        for row in range(rank):
            out[row // share, row % share] = value[row : row + 1]
        for step in range(1, replicas):
            copy(out.at[lax.rem(me + step, replicas)], into, stage, step, me).start()
        into[me] = out[me]

    def end_sum(out, into, gathered, stage):
        for step in range(1, replicas):
            origin = lax.rem(me + replicas - step, replicas)
            copy(out.at[0], into, stage, step, origin).wait_recv()
        total = into[0]
        for origin in range(1, replicas):
            total += into[origin]
        gathered[me] = total * (1.0 / replicas)
        for step in range(1, replicas):
            copy(gathered.at[me], gathered, stage + 1, step, me).start()

    def collect(gathered, stage):
        for step in range(1, replicas):
            origin = lax.rem(me + replicas - step, replicas)
            copy(gathered.at[me], gathered, stage + 1, step, origin).wait_recv()
        return jnp.concatenate(
            [gathered[row // share, row % share] for row in range(rank)], axis=0
        )

    left_local = lax.dot_general(
        q_rows[...], merged[...], (((1,), (1,)), ((), ())),
        precision=highest, preferred_element_type=f32,
    )
    begin_sum(left_local, left_out, left_in, 0)
    end_sum(left_out, left_in, left_all, 0)
    left_sum = collect(left_all, 0)

    right_local = jnp.dot(left_sum, merged[...], precision=highest, preferred_element_type=f32)
    begin_sum(right_local, right_out, right_in, 2)

    gram = lax.dot_general(
        left_sum, left_sum, (((1,), (1,)), ((), ())),
        precision=highest, preferred_element_type=f32,
    )
    rows = lax.broadcasted_iota(jnp.int32, (rank, rank), 0)
    cols = lax.broadcasted_iota(jnp.int32, (rank, rank), 1)
    unit = jnp.where(rows == cols, 1.0, 0.0)
    row_of = lax.broadcasted_iota(jnp.int32, (rank, 1), 0)
    inverse = unit
    pivots = jnp.zeros((rank, 1), f32)
    for k in range(rank):
        pivot = gram[k : k + 1, k : k + 1]
        pivots = jnp.where(row_of == k, pivot, pivots)
        ratio = jnp.where(row_of > k, gram[:, k : k + 1] / pivot, 0.0)
        gram, inverse = gram - ratio * gram[k : k + 1], inverse - ratio * inverse[k : k + 1]
    inverse = inverse / jnp.sqrt(pivots)
    basis = jnp.dot(inverse, left_sum, precision=highest, preferred_element_type=f32)

    end_sum(right_out, right_in, right_all, 2)
    right_sum = collect(right_all, 2)
    q_new = jnp.dot(inverse, right_sum, precision=highest, preferred_element_type=f32)
    q_next[...] = q_new
    approx = lax.dot_general(
        basis, q_new, (((0,), (0,)), ((), ())), precision=highest, preferred_element_type=f32
    )
    new_error[...] = (merged[...] - approx).astype(bf16)

    for stage, source in enumerate((left_out, left_all, right_out, right_all)):
        for step in range(1, replicas):
            copy(source.at[0], source, stage, step, me).wait_send()


def shards(cotangent, route_weights, expert_ids, slot_index, hidden, carried_error, q_factor):
    peers = lax.axis_size("expert")
    replicas = lax.axis_size("dp")
    nx = X_CHIPS
    nz = peers // nx
    half = nz // 2
    tokens, model_dim = cotangent.shape[1:]
    capacity, ff = hidden.shape[2:]
    send = capacity // peers
    width = model_dim // PARTS
    vmem = pl.BlockSpec(memory_space=pltpu.VMEM)
    anywhere = pl.BlockSpec(memory_space=pl.ANY)
    dma = pltpu.SemaphoreType.DMA
    merged = pl.pallas_call(
        functools.partial(route_kernel, nz, nx, send),
        out_shape=jax.ShapeDtypeStruct((ff, model_dim), f32),
        in_specs=[vmem] * 4 + [anywhere] * 2,
        out_specs=vmem,
        scratch_shapes=[
            pltpu.VMEM((2, half, PARTS, tokens, width), bf16),
            pltpu.VMEM((2, half + 1, 16, 128), f32),
            pltpu.VMEM((32, 128), f32),
            pltpu.VMEM((half - 1, PARTS, nx, 2 * send, width), bf16),
            pltpu.VMEM((half - 1, PARTS, nx, 2 * send, width), bf16),
        ]
        + [pltpu.VMEM((PARTS, nx, PAD, width), bf16)] * 4
        + [
            pltpu.VMEM((nz, nx * send, ff), bf16),
            pltpu.VMEM((ff, model_dim), bf16),
            dma((2,)),
            dma((2, half, PARTS)),
            dma((2, half, PARTS)),
            dma((2, half)),
            dma((2, half)),
            dma((half + 1, PARTS, nx - 1)),
            dma((half + 1, PARTS, nx - 1)),
        ],
        compiler_params=pltpu.CompilerParams(
            collective_id=0, has_side_effects=True, vmem_limit_bytes=48 * 1024 * 1024
        ),
        name="route",
    )(
        cotangent[0],
        route_weights[0],
        expert_ids[0],
        slot_index[0],
        hidden[0, 0].reshape(nz, nx * send, ff),
        carried_error[0, 0],
    )
    rank = q_factor.shape[1]
    share = rank // replicas
    new_error, q_next = pl.pallas_call(
        functools.partial(factor_kernel, replicas),
        out_shape=(
            jax.ShapeDtypeStruct((ff, model_dim), bf16),
            jax.ShapeDtypeStruct((rank, model_dim), f32),
        ),
        in_specs=[vmem] * 2,
        out_specs=(vmem, vmem),
        scratch_shapes=[pltpu.VMEM((replicas, share, 1, ff), f32)] * 3
        + [pltpu.VMEM((replicas, share, 1, model_dim), f32)] * 3
        + [dma((4, replicas - 1 if replicas > 1 else 1))] * 2,
        compiler_params=pltpu.CompilerParams(
            collective_id=1, has_side_effects=True, vmem_limit_bytes=48 * 1024 * 1024
        ),
        name="factor",
    )(merged, q_factor[0])
    return (new_error[None, None], q_next[None])


def solution(mesh):
    return jax.shard_map(
        shards,
        mesh=mesh,
        in_specs=(
            P("dp", "expert", None),
            P("dp", "expert", None),
            P("dp", "expert", None),
            P("dp", "expert", None),
            P("dp", "expert", None, None),
            P("dp", "expert", None, None),
            P("expert", None, None),
        ),
        out_specs=(P("dp", "expert", None, None), P("expert", None, None)),
        check_vma=False,
    )
```

time: 291 us -> 136 us (0.47); the launches traced: 288 us -> 136 us
  waiting for transfers between devices: 140 us -> 0 us
  Pallas kernels: 0 us -> 128 us
  blocking collectives: 94.4 us -> 0 us
  starting transfers between devices: 23.1 us -> 0 us
  other arithmetic: 17.6 us -> 0 us
  matrix products: 8.71 us -> 0 us
  local copies, waits for them, and re-layouts: 3.34 us -> 7.32 us
    all_to_all x1 -> x0, waiting for transfers between devices: 140 us -> none  [shards(): lax.all_to_all(outgoing, 'expert', split_axis=0, concat_axis=0, tiled=True)]
    pallas_call x0 -> x2, Pallas kernels: none -> 128 us  [the longest x1 91.5 us: shards(): pl.pallas_call(functools.partial(route_kernel, nz, nx, send), out_shape=j...]
    psum x2 -> x0, blocking collectives: 94.4 us -> none  [the longest x1 48.6 us: shards(): left_sum = lax.psum(left_local, 'dp') / replicas]
    all_to_all x1 -> x0, starting transfers between devices: 23.1 us -> none  [shards(): lax.all_to_all(outgoing, 'expert', split_axis=0, concat_axis=0, tiled=True)]
    scatter x1 -> x0, other arithmetic: 10.3 us -> none  [shards(): outgoing = jnp.zeros((capacity, model_dim), jnp.bfloat16).at[target].set(...]
    dot_general x5 -> x0, matrix products: 8.47 us -> none  [the longest x1 3.76 us: shards(): lax.dot_general(expert_rows, flattened, (((0,), (0,)), ((), ())), preferr...]
    unnamed x11 -> x13, local copies, waits for them, and re-layouts: 2.95 us -> 7.32 us
    another operation x5 -> x0, other arithmetic: 4.01 us -> none  [the longest x3 2.14 us: orthonormal(): lower_factor = jnp.linalg.cholesky(gram_matrix)]
  transfers between devices with their start and end apart: 1 -> 0, of which waited for: 1 -> 0; matrix products, arithmetic and copies ran while one was open for 0% -> 0% of each run, Pallas kernels for 0% -> 0%
where the time goes in v1:
time: 136 us
  Pallas kernels  128 us (94%)
  local copies, waits for them, and re-layouts  7.32 us (5%)
    pallas_call x1, Pallas kernels, shards(): pl.pallas_call(functools.partial(route_kernel, nz, nx, send), out_shape=j...  91.5 us
    pallas_call x1, Pallas kernels, shards(): pl.pallas_call(functools.partial(factor_kernel, replicas), out_shape=(jax...  36.4 us
    unnamed x13, local copies, waits for them, and re-layouts  7.32 us

profile of v1, /device:TPU:1, one launch (start us, length us, event | category | flops | bytes accessed | tf_op | source)
XLA Modules:
  0.0 135.9 jit_solution(1457712128946394711)
XLA Ops:
  0.6 0.8 copy.9
  1.4 0.8 copy.10
  2.3 0.8 copy.11
  3.1 0.0 copy-start
  3.1 1.3 copy-done
  4.3 0.0 copy-start.1
  4.3 1.1 copy-done.1
  5.5 0.0 copy-start.2
  5.5 1.0 copy-done.2
  6.5 0.0 copy-start.3
  6.5 91.5 %route.1.merged = f32[384,1024]{1,0:T(8,128)S(1)} custom-call(bf16[192,1024]{1,0:T(8,128)(2,1)S(1)} %bitcast.12, f32[192,8]{1,0:T(8,128)S(1)} %bitcast.13, s32[192,8]{1,0:T(8,128)S(1)} %bitcast.14, s32[192,8]{1,0:T(8,128)S(1)} %bitcast.15, bf16[16,96,384]{2,1,0:T(8,128)(2,1)S(1)} %bitcast.9, bf16[384,1024]{1,0:T(8,128)(2,1)S(1)} %bitcast.10), custom_call_target="tpu_custom_call" | custom-call | tf_op jit(solution)/shard_map/route/pallas_call | solution.py:370
  98.0 0.0 copy-done.3
  98.0 36.4 %factor.1 = (bf16[384,1024]{1,0:T(8,128)(2,1)S(1)}, f32[16,1024]{1,0:T(8,128)S(1)}) custom-call(f32[384,1024]{1,0:T(8,128)S(1)} %route.1.merged, f32[16,1024]{1,0:T(8,128)S(1)} %bitcast.16), custom_call_target="tpu_custom_call" | custom-call | tf_op jit(solution)/shard_map/factor/pallas_call | solution.py:408
  134.4 0.9 copy.14
  135.3 0.6 copy.15
Async XLA Ops:
  3.1 1.3 copy-start
  4.3 1.1 copy-start.1
  5.5 1.0 copy-start.2
  6.5 91.5 %copy-start.3 = (f32[1,16,1024]{2,1,0:T(8,128)S(1)}, f32[1,16,1024]{2,1,0:T(8,128)}, u32[]{:S(2)}) copy-start(f32[1,16,1024]{2,1,0:T(8,128)} %param.13) | copy-start | bytes 196612

commit v2 on v1

--- a/solution.py
+++ b/solution.py
@@ -14,6 +14,7 @@
 
 X_CHIPS = 4
 PARTS = 4
+VMEM_BYTES = 60 * 1024 * 1024
 PAD = 32
 
 
@@ -23,12 +24,13 @@
     return first, second, value - first - second
 
 
-def route_kernel(
-    nz, nx, send,
-    cot, weights, ids, slots, hidden_hbm, error_hbm, merged,
-    ring, meta, own_meta, picked, arrived, picked_own, arrived_own, picked_far, arrived_far,
+def kernel(
+    nz, nx, send, replicas,
+    cot, weights, ids, slots, hidden_hbm, error_hbm, q_rows, new_error, q_next,
+    merged, splits, own, ring, meta, own_meta, picked, arrived, picked_own, arrived_own, picked_far, arrived_far,
     hidden, error,
-    local_sem, ring_send, ring_recv, meta_send, meta_recv, x_send, x_recv,
+    left_out, left_in, left_all, right_out, right_in, right_all,
+    local_sem, ring_send, ring_recv, meta_send, meta_recv, x_send, x_recv, dp_send, dp_recv,
 ):
     half = nz // 2
     tokens, model_dim = cot.shape
@@ -43,6 +45,8 @@
 
     load_hidden = pltpu.make_async_copy(hidden_hbm, hidden, local_sem.at[0])
     load_error = pltpu.make_async_copy(error_hbm, error, local_sem.at[1])
+    load_own = pltpu.make_async_copy(cot, own, local_sem.at[2])
+    load_own.start()
     load_hidden.start()
     load_error.start()
 
@@ -50,7 +54,11 @@
     partners = [right, left] + [z * nx + lax.rem(x + step, nx) for step in range(1, nx)]
     for partner in partners:
         pl.semaphore_signal(barrier, inc=1, device_id={"expert": partner}, device_id_type=MESH)
-    pl.semaphore_wait(barrier, len(partners))
+    replica = lax.axis_index("dp")
+    for step in range(1, replicas):
+        partner = lax.rem(replica + step, replicas)
+        pl.semaphore_signal(barrier, inc=1, device_id={"dp": partner}, device_id_type=MESH)
+    pl.semaphore_wait(barrier, len(partners) + replicas - 1)
 
     def ring_copy(side, hop, part, source=None):
         return pltpu.make_async_remote_copy(
@@ -91,20 +99,23 @@
         for side in range(2):
             own_copy(side, part).start()
 
-    lane = lax.broadcasted_iota(jnp.int32, (tokens, 128), 1)
-    token = lax.broadcasted_iota(jnp.int32, (tokens, 128), 0).astype(f32)
+    routes = ids.shape[0]
+    spot = lax.broadcasted_iota(jnp.int32, (128, tokens), 0)
+    token = lax.broadcasted_iota(jnp.int32, (128, tokens), 1).astype(f32)
     level = lax.div(ids[...], nx)
     place = lax.rem(ids[...], nx) * send + slots[...]
     to_right = lax.rem(level - z - 1 + 2 * nz, nz)
-    to_left = lax.rem(z - level - 1 + 2 * nz, nz)
-    table = jnp.zeros((128, 512), f32)
-    for k in range(ids.shape[1]):
-        row = (lane == to_right[:, k : k + 1]) | (lane == 16 + to_left[:, k : k + 1])
-        hit = lane == place[:, k : k + 1]
-        values = [token] + list(thirds(jnp.broadcast_to(weights[:, k : k + 1], (tokens, 128))))
-        values = jnp.concatenate([jnp.where(hit, v, 0.0) for v in values], axis=1).astype(bf16)
+    to_left = lax.rem(z - level - 1 + 2 * nz, nz) + 16
+    table = jnp.zeros((32, 512), f32)
+    for k in range(routes):
+        row = (spot[:32] == to_right[k : k + 1]) | (spot[:32] == to_left[k : k + 1])
+        hit = spot == place[k : k + 1]
+        values = [token] + [
+            jnp.broadcast_to(v, (128, tokens)) for v in thirds(weights[k : k + 1, :])
+        ]
+        values = jnp.concatenate([jnp.where(hit, v, 0.0) for v in values], axis=0).astype(bf16)
         table += lax.dot_general(
-            jnp.where(row, 1.0, 0.0).astype(bf16), values, (((0,), (0,)), ((), ())),
+            jnp.where(row, 1.0, 0.0).astype(bf16), values, (((1,), (1,)), ((), ())),
             preferred_element_type=f32,
         )
     which = table[:, :128]
@@ -149,7 +160,7 @@
             pieces += [b[source * send : (source + 1) * send] for b in blocks] + filler
         return jnp.transpose(jnp.concatenate(pieces, axis=0)).astype(bf16)
 
-    def accumulate(land, pick, group, levels, rows, order=range(PARTS)):
+    def accumulate(land, pick, group, levels, rows, order=range(PARTS), then=None):
         turned = hidden_rows(levels, rows)
         for part in order:
             for step in range(1, nx):
@@ -158,6 +169,8 @@
             merged[:, pl.ds(part * width, width)] += jnp.dot(
                 turned, block, preferred_element_type=f32
             )
+            if then is not None:
+                then(part)
 
     def pair_levels(hop):
         return [lax.rem(z - hop + nz, nz), lax.rem(z + hop, nz)]
@@ -185,10 +198,11 @@
     def add_hop(hop):
         accumulate(arrived.at[hop - 1], picked.at[hop - 1], hop - 1, pair_levels(hop), 2 * send)
 
+    load_own.wait()
     got = columns([own_meta[nz - 1 : nz, :], own_meta[nz + 15 : nz + 16, :]])
     own_choice = (one_hot(got[0]), got[1])
     for part in range(PARTS):
-        block = cot[:, part * width : (part + 1) * width]
+        block = own[:, part * width : (part + 1) * width]
         pick_rows([own_choice + (block,)], picked_own, arrived_own, half - 1, part, PAD)
     load_error.wait()
     merged[...] = error[...].astype(f32)
@@ -220,7 +234,72 @@
         pick_rows([far_choice + (block,)], picked_far, arrived_far, half, part, PAD)
     add_hop(half - 1)
     far = lax.rem(z + half, nz)
-    accumulate(arrived_far, picked_far, half, [far], PAD, [part for _, part in order])
+    rank = q_rows.shape[0]
+    ff = merged.shape[0]
+    q_parts = thirds(q_rows[...])
+    blank = jnp.zeros((128 - 3 * rank, model_dim), f32)
+    none = jnp.zeros((rank, model_dim), f32)
+    q_stacks = [
+        jnp.concatenate(list(q_parts[: 3 - i]) + [none] * i + [blank], axis=0).astype(bf16)
+        for i in range(3)
+    ]
+    left_turned = [jnp.zeros((ff, 128), f32)]
+
+    def left_product(part):
+        cols = slice(part * width, (part + 1) * width)
+        for i, piece in enumerate(thirds(merged[:, cols])):
+            piece = piece.astype(bf16)
+            splits[i, :, cols] = piece
+            left_turned[0] += lax.dot_general(
+                piece, q_stacks[i][:, cols], (((1,), (1,)), ((), ())), preferred_element_type=f32
+            )
+
+    accumulate(
+        arrived_far, picked_far, half, [far], PAD, [part for _, part in order], left_product
+    )
+    stacked = jnp.transpose(left_turned[0])
+    left_local = (stacked[2 * rank : 3 * rank] + stacked[rank : 2 * rank]) + stacked[:rank]
+
+    share = rank // replicas
+
+    def dp_copy(source, target, stage, step, origin):
+        return pltpu.make_async_remote_copy(
+            src_ref=source,
+            dst_ref=target.at[origin],
+            send_sem=dp_send.at[stage, step - 1],
+            recv_sem=dp_recv.at[stage, step - 1],
+            device_id={"dp": lax.rem(replica + step, replicas)},
+            device_id_type=MESH,
+        )
+
+    def begin_sum(value, out, into, stage):
+        for row in range(rank):
+            out[row // share, row % share] = value[row : row + 1]
+        for step in range(1, replicas):
+            target = lax.rem(replica + step, replicas)
+            dp_copy(out.at[target], into, stage, step, replica).start()
+        into[replica] = out[replica]
+
+    def end_sum(out, into, gathered, stage):
+        for step in range(1, replicas):
+            origin = lax.rem(replica + replicas - step, replicas)
+            dp_copy(out.at[0], into, stage, step, origin).wait_recv()
+        total = into[0]
+        for origin in range(1, replicas):
+            total += into[origin]
+        gathered[replica] = total * (1.0 / replicas)
+        for step in range(1, replicas):
+            dp_copy(gathered.at[replica], gathered, stage + 1, step, replica).start()
+
+    def collect(gathered, stage):
+        for step in range(1, replicas):
+            origin = lax.rem(replica + replicas - step, replicas)
+            dp_copy(gathered.at[replica], gathered, stage + 1, step, origin).wait_recv()
+        return jnp.concatenate(
+            [gathered[row // share, row % share] for row in range(rank)], axis=0
+        )
+
+    begin_sum(left_local, left_out, left_in, 0)
 
     for part in range(PARTS):
         for side in range(2):
@@ -256,70 +335,17 @@
             for step in range(1, nx):
                 x_copy(pick, land, group, part, step).wait_send()
 
-
-def factor_kernel(
-    replicas,
-    merged, q_rows, new_error, q_next,
-    left_out, left_in, left_all, right_out, right_in, right_all, send_sem, recv_sem,
-):
-    me = lax.axis_index("dp")
-    rank = q_rows.shape[0]
-
-    if replicas > 1:
-        barrier = pltpu.get_barrier_semaphore()
-        for step in range(1, replicas):
-            pl.semaphore_signal(
-                barrier, inc=1, device_id={"dp": lax.rem(me + step, replicas)}, device_id_type=MESH
-            )
-        pl.semaphore_wait(barrier, replicas - 1)
-
-    share = rank // replicas
-
-    def copy(source, target, stage, step, origin):
-        return pltpu.make_async_remote_copy(
-            src_ref=source,
-            dst_ref=target.at[origin],
-            send_sem=send_sem.at[stage, step - 1],
-            recv_sem=recv_sem.at[stage, step - 1],
-            device_id={"dp": lax.rem(me + step, replicas)},
-            device_id_type=MESH,
-        )
-
-    def begin_sum(value, out, into, stage):
-        for row in range(rank):
-            out[row // share, row % share] = value[row : row + 1]
-        for step in range(1, replicas):
-            copy(out.at[lax.rem(me + step, replicas)], into, stage, step, me).start()
-        into[me] = out[me]
-
-    def end_sum(out, into, gathered, stage):
-        for step in range(1, replicas):
-            origin = lax.rem(me + replicas - step, replicas)
-            copy(out.at[0], into, stage, step, origin).wait_recv()
-        total = into[0]
-        for origin in range(1, replicas):
-            total += into[origin]
-        gathered[me] = total * (1.0 / replicas)
-        for step in range(1, replicas):
-            copy(gathered.at[me], gathered, stage + 1, step, me).start()
-
-    def collect(gathered, stage):
-        for step in range(1, replicas):
-            origin = lax.rem(me + replicas - step, replicas)
-            copy(gathered.at[me], gathered, stage + 1, step, origin).wait_recv()
-        return jnp.concatenate(
-            [gathered[row // share, row % share] for row in range(rank)], axis=0
-        )
-
-    left_local = lax.dot_general(
-        q_rows[...], merged[...], (((1,), (1,)), ((), ())),
-        precision=highest, preferred_element_type=f32,
-    )
-    begin_sum(left_local, left_out, left_in, 0)
     end_sum(left_out, left_in, left_all, 0)
     left_sum = collect(left_all, 0)
 
-    right_local = jnp.dot(left_sum, merged[...], precision=highest, preferred_element_type=f32)
+    left_parts = thirds(left_sum)
+    left_stack = jnp.concatenate(left_parts, axis=0).astype(bf16)
+    right_local = None
+    for i in (2, 1, 0):
+        product = jnp.dot(left_stack[: (3 - i) * rank], splits[i], preferred_element_type=f32)
+        for j in range(2 - i, -1, -1):
+            term = product[j * rank : (j + 1) * rank]
+            right_local = term if right_local is None else right_local + term
     begin_sum(right_local, right_out, right_in, 2)
 
     gram = lax.dot_general(
@@ -328,9 +354,8 @@
     )
     rows = lax.broadcasted_iota(jnp.int32, (rank, rank), 0)
     cols = lax.broadcasted_iota(jnp.int32, (rank, rank), 1)
-    unit = jnp.where(rows == cols, 1.0, 0.0)
     row_of = lax.broadcasted_iota(jnp.int32, (rank, 1), 0)
-    inverse = unit
+    inverse = jnp.where(rows == cols, 1.0, 0.0)
     pivots = jnp.zeros((rank, 1), f32)
     for k in range(rank):
         pivot = gram[k : k + 1, k : k + 1]
@@ -339,19 +364,23 @@
         gram, inverse = gram - ratio * gram[k : k + 1], inverse - ratio * inverse[k : k + 1]
     inverse = inverse / jnp.sqrt(pivots)
     basis = jnp.dot(inverse, left_sum, precision=highest, preferred_element_type=f32)
+    b1, b2, b3 = thirds(basis)
+    basis_stack = jnp.transpose(jnp.concatenate([b1, b1, b1, b2, b2, b3], axis=0)).astype(bf16)
 
     end_sum(right_out, right_in, right_all, 2)
     right_sum = collect(right_all, 2)
     q_new = jnp.dot(inverse, right_sum, precision=highest, preferred_element_type=f32)
     q_next[...] = q_new
-    approx = lax.dot_general(
-        basis, q_new, (((0,), (0,)), ((), ())), precision=highest, preferred_element_type=f32
-    )
-    new_error[...] = (merged[...] - approx).astype(bf16)
+    p1, p2, p3 = thirds(q_new)
+    q_stack = jnp.concatenate([p1, p2, p3, p1, p2, p1], axis=0).astype(bf16)
+    for part in range(PARTS):
+        cols = slice(part * width, (part + 1) * width)
+        approx = jnp.dot(basis_stack, q_stack[:, cols], preferred_element_type=f32)
+        new_error[:, cols] = (merged[:, cols] - approx).astype(bf16)
 
     for stage, source in enumerate((left_out, left_all, right_out, right_all)):
         for step in range(1, replicas):
-            copy(source.at[0], source, stage, step, me).wait_send()
+            dp_copy(source.at[0], source, stage, step, replica).wait_send()
 
 
 def shards(cotangent, route_weights, expert_ids, slot_index, hidden, carried_error, q_factor):
@@ -367,12 +396,20 @@
     vmem = pl.BlockSpec(memory_space=pltpu.VMEM)
     anywhere = pl.BlockSpec(memory_space=pl.ANY)
     dma = pltpu.SemaphoreType.DMA
-    merged = pl.pallas_call(
-        functools.partial(route_kernel, nz, nx, send),
-        out_shape=jax.ShapeDtypeStruct((ff, model_dim), f32),
-        in_specs=[vmem] * 4 + [anywhere] * 2,
-        out_specs=vmem,
+    rank = q_factor.shape[1]
+    share = rank // replicas
+    new_error, q_next = pl.pallas_call(
+        functools.partial(kernel, nz, nx, send, replicas),
+        out_shape=(
+            jax.ShapeDtypeStruct((ff, model_dim), bf16),
+            jax.ShapeDtypeStruct((rank, model_dim), f32),
+        ),
+        in_specs=[anywhere] + [vmem] * 3 + [anywhere] * 2 + [vmem],
+        out_specs=(vmem, vmem),
         scratch_shapes=[
+            pltpu.VMEM((ff, model_dim), f32),
+            pltpu.VMEM((3, ff, model_dim), bf16),
+            pltpu.VMEM((tokens, model_dim), bf16),
             pltpu.VMEM((2, half, PARTS, tokens, width), bf16),
             pltpu.VMEM((2, half + 1, 16, 128), f32),
             pltpu.VMEM((32, 128), f32),
@@ -383,44 +420,33 @@
         + [
             pltpu.VMEM((nz, nx * send, ff), bf16),
             pltpu.VMEM((ff, model_dim), bf16),
-            dma((2,)),
+        ]
+        + [pltpu.VMEM((replicas, share, 1, ff), f32)] * 3
+        + [pltpu.VMEM((replicas, share, 1, model_dim), f32)] * 3
+        + [
+            dma((3,)),
             dma((2, half, PARTS)),
             dma((2, half, PARTS)),
             dma((2, half)),
             dma((2, half)),
             dma((half + 1, PARTS, nx - 1)),
             dma((half + 1, PARTS, nx - 1)),
+            dma((4, max(replicas - 1, 1))),
+            dma((4, max(replicas - 1, 1))),
         ],
         compiler_params=pltpu.CompilerParams(
-            collective_id=0, has_side_effects=True, vmem_limit_bytes=48 * 1024 * 1024
+            collective_id=0, has_side_effects=True, vmem_limit_bytes=VMEM_BYTES
         ),
-        name="route",
+        name="route_and_factor",
     )(
         cotangent[0],
-        route_weights[0],
-        expert_ids[0],
-        slot_index[0],
+        route_weights[0].T,
+        expert_ids[0].T,
+        slot_index[0].T,
         hidden[0, 0].reshape(nz, nx * send, ff),
         carried_error[0, 0],
+        q_factor[0],
     )
-    rank = q_factor.shape[1]
-    share = rank // replicas
-    new_error, q_next = pl.pallas_call(
-        functools.partial(factor_kernel, replicas),
-        out_shape=(
-            jax.ShapeDtypeStruct((ff, model_dim), bf16),
-            jax.ShapeDtypeStruct((rank, model_dim), f32),
-        ),
-        in_specs=[vmem] * 2,
-        out_specs=(vmem, vmem),
-        scratch_shapes=[pltpu.VMEM((replicas, share, 1, ff), f32)] * 3
-        + [pltpu.VMEM((replicas, share, 1, model_dim), f32)] * 3
-        + [dma((4, replicas - 1 if replicas > 1 else 1))] * 2,
-        compiler_params=pltpu.CompilerParams(
-            collective_id=1, has_side_effects=True, vmem_limit_bytes=48 * 1024 * 1024
-        ),
-        name="factor",
-    )(merged, q_factor[0])
     return (new_error[None, None], q_next[None])
 
 

time: 136 us -> 128 us (0.941)
  local copies, waits for them, and re-layouts: 7.32 us -> 2.73 us
  Pallas kernels: 128 us -> 125 us
    unnamed x13 -> x4, local copies, waits for them, and re-layouts: 7.32 us -> 2.73 us
    pallas_call x2 -> x1, Pallas kernels: 128 us -> 125 us  [shards(): pl.pallas_call(functools.partial(kernel, nz, nx, send, replicas), out_sha...]
where the time goes in v2:
time: 128 us
  Pallas kernels  125 us (98%)
  local copies, waits for them, and re-layouts  2.73 us (2%)
    pallas_call x1, Pallas kernels, shards(): pl.pallas_call(functools.partial(kernel, nz, nx, send, replicas), out_sha...  125 us
    unnamed x4, local copies, waits for them, and re-layouts  2.73 us

profile of v2, /device:TPU:1, one launch (start us, length us, event | category | flops | bytes accessed | tf_op | source)
XLA Modules:
  0.0 128.2 jit_solution(15353579532373084511)
XLA Ops:
  0.6 124.8 %route_and_factor.1 = (bf16[384,1024]{1,0:T(8,128)(2,1)}, f32[16,1024]{1,0:T(8,128)}) custom-call(bf16[192,1024]{1,0:T(8,128)(2,1)} %bitcast.18, f32[8,192]{1,0:T(8,128)} %bitcast.21, s32[8,192]{1,0:T(8,128)} %bitcast.22, s32[8,192]{1,0:T(8,128)} %bitcast.23, bf16[16,96,384]{2,1,0:T(8,128)(2,1)} %bitcast.15, bf16[384,1024]{1,0:T(8,128)(2,1)} %bitcast.17, ...), custom_call_target="tpu_custom_call" | custom-call | tf_op jit(solution)/shard_map/route_and_factor/pallas_call | solution.py:401
  125.5 0.0 copy-start
  125.5 2.1 %copy.11 = bf16[1,1,384,1024]{3,2,1,0:T(8,128)(2,1)} copy(bf16[1,1,384,1024]{3,2,1,0:T(8,128)(2,1)} %bitcast.16) | data formatting | bytes 1572864
  127.6 0.0 copy-done
  127.6 0.6 copy.12
Async XLA Ops:
  125.5 2.1 %copy-start = (f32[16,1024]{1,0:T(8,128)S(1)}, f32[16,1024]{1,0:T(8,128)}, u32[]{:S(2)}) copy-start(f32[16,1024]{1,0:T(8,128)} %get-tuple-element.5) | copy-start | bytes 196612

commit v3 on v2

--- a/solution.py
+++ b/solution.py
@@ -14,7 +14,8 @@
 
 X_CHIPS = 4
 PARTS = 4
-VMEM_BYTES = 60 * 1024 * 1024
+VMEM_BYTES = 56 * 1024 * 1024
+STEPS = 4
 PAD = 32
 
 
@@ -26,7 +27,8 @@
 
 def kernel(
     nz, nx, send, replicas,
-    cot, weights, ids, slots, hidden_hbm, error_hbm, q_rows, new_error, q_next,
+    cot, weights, ids, slots, hidden_hbm, error_hbm, q_rows,
+    merged_hbm, basis_stack, q_stack, q_next,
     merged, splits, own, ring, meta, own_meta, picked, arrived, picked_own, arrived_own, picked_far, arrived_far,
     hidden, error,
     left_out, left_in, left_all, right_out, right_in, right_all,
@@ -47,8 +49,6 @@
     load_error = pltpu.make_async_copy(error_hbm, error, local_sem.at[1])
     load_own = pltpu.make_async_copy(cot, own, local_sem.at[2])
     load_own.start()
-    load_hidden.start()
-    load_error.start()
 
     barrier = pltpu.get_barrier_semaphore()
     partners = [right, left] + [z * nx + lax.rem(x + step, nx) for step in range(1, nx)]
@@ -71,7 +71,7 @@
         )
 
     def own_copy(side, part):
-        return ring_copy(side, 1, part, cot.at[:, pl.ds(part * width, width)])
+        return ring_copy(side, 1, part, own.at[:, pl.ds(part * width, width)])
 
     def meta_copy(side, hop):
         return pltpu.make_async_remote_copy(
@@ -95,9 +95,12 @@
             device_id_type=MESH,
         )
 
+    load_own.wait()
     for part in range(PARTS):
         for side in range(2):
             own_copy(side, part).start()
+    load_hidden.start()
+    load_error.start()
 
     routes = ids.shape[0]
     spot = lax.broadcasted_iota(jnp.int32, (128, tokens), 0)
@@ -179,7 +182,7 @@
         choices = None
         for part in range(PARTS):
             for side in range(2):
-                ring_copy(side, hop, part, cot.at[:, pl.ds(0, width)]).wait_recv()
+                ring_copy(side, hop, part, own.at[:, pl.ds(0, width)]).wait_recv()
                 if forward(side, part):
                     ring_copy(side, hop + 1, part).start()
             if choices is None:
@@ -198,7 +201,24 @@
     def add_hop(hop):
         accumulate(arrived.at[hop - 1], picked.at[hop - 1], hop - 1, pair_levels(hop), 2 * send)
 
-    load_own.wait()
+    everything = lambda side, part: True
+    last = lambda side, part: (side == 0) if part is None else (part < PARTS // 2) == (side == 0)
+    def drain_ring(hop, sent=everything):
+        for part in range(PARTS):
+            for side in range(2):
+                if sent(side, part):
+                    ring_copy(side, hop, part).wait_send()
+        for side in range(2):
+            if sent(side, None):
+                meta_copy(side, hop).wait_send()
+
+    def drain_x(group, pick=None, land=None):
+        pick = picked.at[group] if pick is None else pick
+        land = arrived.at[group] if land is None else land
+        for part in range(PARTS):
+            for step in range(1, nx):
+                x_copy(pick, land, group, part, step).wait_send()
+
     got = columns([own_meta[nz - 1 : nz, :], own_meta[nz + 15 : nz + 16, :]])
     own_choice = (one_hot(got[0]), got[1])
     for part in range(PARTS):
@@ -208,19 +228,26 @@
     merged[...] = error[...].astype(f32)
     load_hidden.wait()
 
-    everything = lambda side, part: True
-    last = lambda side, part: (side == 0) if part is None else (part < PARTS // 2) == (side == 0)
     step_hop(1, everything)
     accumulate(arrived_own, picked_own, half - 1, [z], PAD)
+    for part in range(PARTS):
+        for side in range(2):
+            own_copy(side, part).wait_send()
+    for side in range(2):
+        meta_copy(side, 1).wait_send()
 
     def body(hop, carry):
         step_hop(hop, everything)
         add_hop(hop - 1)
+        drain_ring(hop)
+        drain_x(hop - 2)
         return carry
 
     lax.fori_loop(2, half - 1, body, 0)
     step_hop(half - 1, last)
     add_hop(half - 2)
+    drain_ring(half - 1)
+    drain_x(half - 3)
 
     meta_copy(0, half).wait_recv()
     got = columns([meta[0, half, half - 1 : half, :], meta[0, half, half + 7 : half + 8, :]])
@@ -229,7 +256,7 @@
     for part in range(PARTS // 2):
         order += [(0, part), (1, part + PARTS // 2)]
     for side, part in order:
-        ring_copy(side, half, part, cot.at[:, pl.ds(0, width)]).wait_recv()
+        ring_copy(side, half, part, own.at[:, pl.ds(0, width)]).wait_recv()
         block = ring[side, half - 1, part]
         pick_rows([far_choice + (block,)], picked_far, arrived_far, half, part, PAD)
     add_hop(half - 1)
@@ -275,65 +302,46 @@
     def begin_sum(value, out, into, stage):
         for row in range(rank):
             out[row // share, row % share] = value[row : row + 1]
-        for step in range(1, replicas):
+        @pl.loop(1, replicas)
+        def _(step):
             target = lax.rem(replica + step, replicas)
             dp_copy(out.at[target], into, stage, step, replica).start()
+
         into[replica] = out[replica]
 
     def end_sum(out, into, gathered, stage):
-        for step in range(1, replicas):
+        @pl.loop(1, replicas)
+        def _(step):
             origin = lax.rem(replica + replicas - step, replicas)
             dp_copy(out.at[0], into, stage, step, origin).wait_recv()
+
         total = into[0]
         for origin in range(1, replicas):
             total += into[origin]
         gathered[replica] = total * (1.0 / replicas)
-        for step in range(1, replicas):
+
+        @pl.loop(1, replicas)
+        def _(step):
             dp_copy(gathered.at[replica], gathered, stage + 1, step, replica).start()
 
     def collect(gathered, stage):
-        for step in range(1, replicas):
+        @pl.loop(1, replicas)
+        def _(step):
             origin = lax.rem(replica + replicas - step, replicas)
             dp_copy(gathered.at[replica], gathered, stage + 1, step, origin).wait_recv()
+
         return jnp.concatenate(
             [gathered[row // share, row % share] for row in range(rank)], axis=0
         )
 
     begin_sum(left_local, left_out, left_in, 0)
-
-    for part in range(PARTS):
-        for side in range(2):
-            own_copy(side, part).wait_send()
-    for side in range(2):
-        meta_copy(side, 1).wait_send()
-
-    def drain(hop, carry):
-        for part in range(PARTS):
-            for side in range(2):
-                ring_copy(side, hop, part).wait_send()
-        for side in range(2):
-            meta_copy(side, hop).wait_send()
-        return carry
-
-    lax.fori_loop(2, half, drain, 0)
-    for side, part in order:
-        ring_copy(side, half, part).wait_send()
-    meta_copy(0, half).wait_send()
-
-    def drain_x(group, carry):
-        for part in range(PARTS):
-            for step in range(1, nx):
-                x_copy(picked.at[group], arrived.at[group], group, part, step).wait_send()
-        return carry
-
-    lax.fori_loop(0, half - 1, drain_x, 0)
-    for pick, land, group in (
-        (picked_own, arrived_own, half - 1),
-        (picked_far, arrived_far, half),
-    ):
-        for part in range(PARTS):
-            for step in range(1, nx):
-                x_copy(pick, land, group, part, step).wait_send()
+    save_merged = pltpu.make_async_copy(merged, merged_hbm, local_sem.at[3])
+    save_merged.start()
+
+    drain_ring(half, last)
+    drain_x(half - 2)
+    drain_x(half - 1, picked_own, arrived_own)
+    drain_x(half, picked_far, arrived_far)
 
     end_sum(left_out, left_in, left_all, 0)
     left_sum = collect(left_all, 0)
@@ -365,22 +373,29 @@
     inverse = inverse / jnp.sqrt(pivots)
     basis = jnp.dot(inverse, left_sum, precision=highest, preferred_element_type=f32)
     b1, b2, b3 = thirds(basis)
-    basis_stack = jnp.transpose(jnp.concatenate([b1, b1, b1, b2, b2, b3], axis=0)).astype(bf16)
+    blank = jnp.zeros((128 - 6 * rank, ff), f32)
+    basis_stack[...] = jnp.transpose(
+        jnp.concatenate([b1, b1, b1, b2, b2, b3, blank], axis=0)
+    ).astype(bf16)
 
     end_sum(right_out, right_in, right_all, 2)
     right_sum = collect(right_all, 2)
     q_new = jnp.dot(inverse, right_sum, precision=highest, preferred_element_type=f32)
     q_next[...] = q_new
     p1, p2, p3 = thirds(q_new)
-    q_stack = jnp.concatenate([p1, p2, p3, p1, p2, p1], axis=0).astype(bf16)
-    for part in range(PARTS):
-        cols = slice(part * width, (part + 1) * width)
-        approx = jnp.dot(basis_stack, q_stack[:, cols], preferred_element_type=f32)
-        new_error[:, cols] = (merged[:, cols] - approx).astype(bf16)
-
+    blank = jnp.zeros((128 - 6 * rank, model_dim), f32)
+    q_stack[...] = jnp.concatenate([p1, p2, p3, p1, p2, p1, blank], axis=0).astype(bf16)
+    save_merged.wait()
     for stage, source in enumerate((left_out, left_all, right_out, right_all)):
-        for step in range(1, replicas):
+        @pl.loop(1, replicas)
+        def _(step):
             dp_copy(source.at[0], source, stage, step, replica).wait_send()
+
+
+def apply_kernel(merged, basis_stack, q_stack, q_new, new_error, q_next):
+    approx = jnp.dot(basis_stack[...], q_stack[...], preferred_element_type=f32)
+    new_error[...] = (merged[...] - approx).astype(bf16)
+    q_next[...] = q_new[...]
 
 
 def shards(cotangent, route_weights, expert_ids, slot_index, hidden, carried_error, q_factor):
@@ -394,18 +409,20 @@
     send = capacity // peers
     width = model_dim // PARTS
     vmem = pl.BlockSpec(memory_space=pltpu.VMEM)
-    anywhere = pl.BlockSpec(memory_space=pl.ANY)
+    hbm = pl.BlockSpec(memory_space=pltpu.HBM)
     dma = pltpu.SemaphoreType.DMA
     rank = q_factor.shape[1]
     share = rank // replicas
-    new_error, q_next = pl.pallas_call(
+    merged, basis_stack, q_stack, q_new = pl.pallas_call(
         functools.partial(kernel, nz, nx, send, replicas),
         out_shape=(
-            jax.ShapeDtypeStruct((ff, model_dim), bf16),
+            jax.ShapeDtypeStruct((ff, model_dim), f32),
+            jax.ShapeDtypeStruct((ff, 128), bf16),
+            jax.ShapeDtypeStruct((128, model_dim), bf16),
             jax.ShapeDtypeStruct((rank, model_dim), f32),
         ),
-        in_specs=[anywhere] + [vmem] * 3 + [anywhere] * 2 + [vmem],
-        out_specs=(vmem, vmem),
+        in_specs=[hbm] + [vmem] * 3 + [hbm] * 2 + [vmem],
+        out_specs=(hbm, vmem, vmem, vmem),
         scratch_shapes=[
             pltpu.VMEM((ff, model_dim), f32),
             pltpu.VMEM((3, ff, model_dim), bf16),
@@ -424,7 +441,7 @@
         + [pltpu.VMEM((replicas, share, 1, ff), f32)] * 3
         + [pltpu.VMEM((replicas, share, 1, model_dim), f32)] * 3
         + [
-            dma((3,)),
+            dma((4,)),
             dma((2, half, PARTS)),
             dma((2, half, PARTS)),
             dma((2, half)),
@@ -447,6 +464,27 @@
         carried_error[0, 0],
         q_factor[0],
     )
+    rows = ff // STEPS
+    new_error, q_next = pl.pallas_call(
+        apply_kernel,
+        grid=(STEPS,),
+        out_shape=(
+            jax.ShapeDtypeStruct((ff, model_dim), bf16),
+            jax.ShapeDtypeStruct((rank, model_dim), f32),
+        ),
+        in_specs=[
+            pl.BlockSpec((rows, model_dim), lambda i: (i, 0)),
+            pl.BlockSpec((rows, 128), lambda i: (i, 0)),
+            pl.BlockSpec((128, model_dim), lambda i: (0, 0)),
+            pl.BlockSpec((rank, model_dim), lambda i: (0, 0)),
+        ],
+        out_specs=(
+            pl.BlockSpec((rows, model_dim), lambda i: (i, 0)),
+            pl.BlockSpec((rank, model_dim), lambda i: (0, 0)),
+        ),
+        compiler_params=pltpu.CompilerParams(vmem_limit_bytes=VMEM_BYTES),
+        name="apply_factors",
+    )(merged, basis_stack, q_stack, q_new)
     return (new_error[None, None], q_next[None])
 
 

time: 128 us -> 128 us (level)
  local copies, waits for them, and re-layouts: 2.73 us -> 0 us
  Pallas kernels: 125 us -> 127 us
    pallas_call x0 -> x1, Pallas kernels: none -> 3.89 us  [shards(): pl.pallas_call(apply_kernel, grid=(STEPS,), out_shape=(jax.ShapeDtypeStru...]
    unnamed x4 -> x0, local copies, waits for them, and re-layouts: 2.73 us -> none
    pallas_call x1, Pallas kernels: 125 us -> 123 us  [shards(): pl.pallas_call(functools.partial(kernel, nz, nx, send, replicas), out_sha...]
where the time goes in v3:
time: 128 us
  Pallas kernels  127 us (99%)
    pallas_call x1, Pallas kernels, shards(): pl.pallas_call(functools.partial(kernel, nz, nx, send, replicas), out_sha...  123 us
    pallas_call x1, Pallas kernels, shards(): pl.pallas_call(apply_kernel, grid=(STEPS,), out_shape=(jax.ShapeDtypeStru...  3.89 us

profile of v3, /device:TPU:1, one launch (start us, length us, event | category | flops | bytes accessed | tf_op | source)
XLA Modules:
  0.0 127.8 jit_solution(17435947810605944550)
XLA Ops:
  0.6 123.3 %route_and_factor.1 = (f32[384,1024]{1,0:T(8,128)}, bf16[384,128]{1,0:T(8,128)(2,1)}, bf16[128,1024]{1,0:T(8,128)(2,1)}, f32[16,1024]{1,0:T(8,128)}) custom-call(bf16[192,1024]{1,0:T(8,128)(2,1)} %bitcast.17, f32[8,192]{1,0:T(8,128)} %bitcast.19, s32[8,192]{1,0:T(8,128)} %bitcast.20, s32[8,192]{1,0:T(8,128)} %bitcast.21, bf16[16,96,384]{2,1,0:T(8,128)(2,1)} %bitcast.15, ...), custom_call_target="tpu_custom_call" | custom-call | tf_op jit(solution)/shard_map/route_and_factor/pallas_call | solution.py:416
  123.9 3.9 %apply_factors.1 = (bf16[384,1024]{1,0:T(8,128)(2,1)}, f32[16,1024]{1,0:T(8,128)}) custom-call(f32[384,1024]{1,0:T(8,128)} %get-tuple-element.8.merged, bf16[384,128]{1,0:T(8,128)(2,1)} %get-tuple-element.9.basis_stack, bf16[128,1024]{1,0:T(8,128)(2,1)} %get-tuple-element.10.q_stack, f32[16,1024]{1,0:T(8,128)} %get-tuple-element.11.q_new), custom_call_target="tpu_custom_call" | custom-call | tf_op jit(solution)/shard_map/apply_factors/pallas_call | solution.py:468

commit v4 on v3

--- a/solution.py
+++ b/solution.py
@@ -29,10 +29,11 @@
     nz, nx, send, replicas,
     cot, weights, ids, slots, hidden_hbm, error_hbm, q_rows,
     merged_hbm, basis_stack, q_stack, q_next,
-    merged, splits, own, ring, meta, own_meta, picked, arrived, picked_own, arrived_own, picked_far, arrived_far,
+    merged, splits, own, ring, meta, own_meta, picked, arrived, picked_own, arrived_own, picked_near, arrived_near, direct_out, direct_in,
     hidden, error,
     left_out, left_in, left_all, right_out, right_in, right_all,
-    local_sem, ring_send, ring_recv, meta_send, meta_recv, x_send, x_recv, dp_send, dp_recv,
+    local_sem, ring_send, ring_recv, meta_send, meta_recv, x_send, x_recv,
+    direct_send, direct_recv, dp_send, dp_recv,
 ):
     half = nz // 2
     tokens, model_dim = cot.shape
@@ -51,7 +52,9 @@
     load_own.start()
 
     barrier = pltpu.get_barrier_semaphore()
-    partners = [right, left] + [z * nx + lax.rem(x + step, nx) for step in range(1, nx)]
+    levels = (lax.rem(z + 1, nz), lax.rem(z + nz - 1, nz))
+    partners = [v * nx + lax.rem(x + step, nx) for step in range(nx) for v in levels]
+    partners += [z * nx + lax.rem(x + step, nx) for step in range(1, nx)]
     for partner in partners:
         pl.semaphore_signal(barrier, inc=1, device_id={"expert": partner}, device_id_type=MESH)
     replica = lax.axis_index("dp")
@@ -95,10 +98,25 @@
             device_id_type=MESH,
         )
 
+    def direct_copy(stage, side, step, source=None):
+        target = lax.rem(x + step, nx)
+        source = x if source is None else source
+        return pltpu.make_async_remote_copy(
+            src_ref=direct_out.at[stage, side, target],
+            dst_ref=direct_in.at[stage, side, source],
+            send_sem=direct_send.at[stage, side, step],
+            recv_sem=direct_recv.at[stage, side, step],
+            device_id={"expert": levels[side] * nx + target},
+            device_id_type=MESH,
+        )
+
     load_own.wait()
-    for part in range(PARTS):
+    turn = PARTS // 2
+    order = [(part, (part + turn) % PARTS) for part in range(PARTS)]
+    kept = (range(turn), range(turn, PARTS))
+    for parts in order:
         for side in range(2):
-            own_copy(side, part).start()
+            own_copy(side, parts[side]).start()
     load_hidden.start()
     load_error.start()
 
@@ -140,7 +158,7 @@
     def one_hot(which_column):
         return jnp.where(token_lane == which_column, 1.0, 0.0).astype(bf16)
 
-    def pick_rows(blocks, pick, land, group, part, rows):
+    def pick_rows(blocks, pick, rows):
         chosen = [
             jnp.dot(choice, block, preferred_element_type=f32) * scale
             for choice, scale, block in blocks
@@ -149,10 +167,19 @@
         filler = [jnp.zeros((pad, width), f32)] if pad else []
         for target in range(nx):
             cut = [c[target * send : (target + 1) * send] for c in chosen]
-            pick[part, target] = jnp.concatenate(cut + filler, axis=0).astype(bf16)
+            pick[target] = jnp.concatenate(cut + filler, axis=0).astype(bf16)
+
+    def pass_rows(pick, land, group, part):
         for step in range(1, nx):
             x_copy(pick, land, group, part, step).start()
         land[part, x] = pick[part, x]
+
+    def choices_of(hop, distance):
+        got = columns(
+            [meta[s, hop, pl.ds(distance - 1, 1), :] for s in range(2)]
+            + [meta[s, hop, pl.ds(distance + 7, 1), :] for s in range(2)]
+        )
+        return [(one_hot(got[s]), got[2 + s]) for s in range(2)]
 
     def hidden_rows(levels, rows):
         blocks = [hidden[v].astype(f32) for v in levels]
@@ -163,104 +190,144 @@
             pieces += [b[source * send : (source + 1) * send] for b in blocks] + filler
         return jnp.transpose(jnp.concatenate(pieces, axis=0)).astype(bf16)
 
-    def accumulate(land, pick, group, levels, rows, order=range(PARTS), then=None):
+    def accumulate(land, pick, group, levels, rows):
         turned = hidden_rows(levels, rows)
-        for part in order:
+        for part in range(PARTS):
             for step in range(1, nx):
                 x_copy(pick, land, group, part, step, lax.rem(x + nx - step, nx)).wait_recv()
             block = land[part].reshape(nx * rows, width)
             merged[:, pl.ds(part * width, width)] += jnp.dot(
                 turned, block, preferred_element_type=f32
             )
-            if then is not None:
-                then(part)
 
     def pair_levels(hop):
         return [lax.rem(z - hop + nz, nz), lax.rem(z + hop, nz)]
 
     def step_hop(hop, forward):
         choices = None
-        for part in range(PARTS):
+        for slot, parts in enumerate(order):
             for side in range(2):
-                ring_copy(side, hop, part, own.at[:, pl.ds(0, width)]).wait_recv()
-                if forward(side, part):
-                    ring_copy(side, hop + 1, part).start()
+                ring_copy(side, hop, parts[side], own.at[:, pl.ds(0, width)]).wait_recv()
+                if forward(side, parts[side]):
+                    ring_copy(side, hop + 1, parts[side]).start()
             if choices is None:
                 for side in range(2):
                     meta_copy(side, hop).wait_recv()
-                    if forward(side, None):
-                        meta_copy(side, hop + 1).start()
-                got = columns(
-                    [meta[s, hop, pl.ds(hop - 1, 1), :] for s in range(2)]
-                    + [meta[s, hop, pl.ds(hop + 7, 1), :] for s in range(2)]
-                )
-                choices = [(one_hot(got[s]), got[2 + s]) for s in range(2)]
-            blocks = [choices[s] + (ring[s, hop - 1, part],) for s in range(2)]
-            pick_rows(blocks, picked.at[hop - 1], arrived.at[hop - 1], hop - 1, part, 2 * send)
+                    meta_copy(side, hop + 1).start()
+                choices = choices_of(hop, hop)
+            if slot >= turn:
+                for part in parts:
+                    blocks = [choices[s] + (ring[s, hop - 1, part],) for s in range(2)]
+                    pick_rows(blocks, picked.at[hop - 1, part], 2 * send)
+                    pass_rows(picked.at[hop - 1], arrived.at[hop - 1], hop - 1, part)
+
+    def send_direct(stage, hop):
+        choices = choices_of(hop, hop + 1)
+        for side in range(2):
+            parts = kept[side] if stage else kept[1 - side]
+            blocks = [choices[side] + (ring[side, hop - 1, part],) for part in parts]
+            pick_rows(blocks, direct_out.at[stage, side], 2 * send)
+            for step in range(nx):
+                direct_copy(stage, side, step).start()
 
     def add_hop(hop):
         accumulate(arrived.at[hop - 1], picked.at[hop - 1], hop - 1, pair_levels(hop), 2 * send)
 
     everything = lambda side, part: True
-    last = lambda side, part: (side == 0) if part is None else (part < PARTS // 2) == (side == 0)
+    going_on = lambda side, part: part in kept[side]
+
     def drain_ring(hop, sent=everything):
         for part in range(PARTS):
             for side in range(2):
                 if sent(side, part):
                     ring_copy(side, hop, part).wait_send()
         for side in range(2):
-            if sent(side, None):
-                meta_copy(side, hop).wait_send()
-
-    def drain_x(group, pick=None, land=None):
-        pick = picked.at[group] if pick is None else pick
-        land = arrived.at[group] if land is None else land
-        for part in range(PARTS):
+            meta_copy(side, hop).wait_send()
+
+    def drain_x(group, pick, land, parts=range(PARTS)):
+        for part in parts:
             for step in range(1, nx):
                 x_copy(pick, land, group, part, step).wait_send()
+
+    def drain_hop(hop):
+        drain_x(hop - 1, picked.at[hop - 1], arrived.at[hop - 1])
 
     got = columns([own_meta[nz - 1 : nz, :], own_meta[nz + 15 : nz + 16, :]])
     own_choice = (one_hot(got[0]), got[1])
     for part in range(PARTS):
         block = own[:, part * width : (part + 1) * width]
-        pick_rows([own_choice + (block,)], picked_own, arrived_own, half - 1, part, PAD)
+        pick_rows([own_choice + (block,)], picked_own.at[part], PAD)
+        pass_rows(picked_own, arrived_own, half - 2, part)
     load_error.wait()
     merged[...] = error[...].astype(f32)
     load_hidden.wait()
 
     step_hop(1, everything)
-    accumulate(arrived_own, picked_own, half - 1, [z], PAD)
+    accumulate(arrived_own, picked_own, half - 2, [z], PAD)
     for part in range(PARTS):
         for side in range(2):
             own_copy(side, part).wait_send()
     for side in range(2):
         meta_copy(side, 1).wait_send()
+    drain_x(half - 2, picked_own, arrived_own)
 
     def body(hop, carry):
         step_hop(hop, everything)
         add_hop(hop - 1)
         drain_ring(hop)
-        drain_x(hop - 2)
+        drain_hop(hop - 1)
         return carry
 
-    lax.fori_loop(2, half - 1, body, 0)
-    step_hop(half - 1, last)
+    lax.fori_loop(2, half - 2, body, 0)
+    step_hop(half - 2, going_on)
+    send_direct(0, half - 2)
+    add_hop(half - 3)
+    drain_ring(half - 2)
+    drain_hop(half - 3)
+
+    for parts in order[:turn]:
+        for side in range(2):
+            ring_copy(side, half - 1, parts[side], own.at[:, pl.ds(0, width)]).wait_recv()
+    for side in range(2):
+        meta_copy(side, half - 1).wait_recv()
+    send_direct(1, half - 1)
+    choices = choices_of(half - 1, half - 1)
+    for side in range(2):
+        blocks = [choices[side] + (ring[side, half - 2, part],) for part in kept[side]]
+        pick_rows(blocks, picked_near.at[side], 2 * send)
+        pass_rows(picked_near, arrived_near, half - 1, side)
     add_hop(half - 2)
-    drain_ring(half - 1)
-    drain_x(half - 3)
-
-    meta_copy(0, half).wait_recv()
-    got = columns([meta[0, half, half - 1 : half, :], meta[0, half, half + 7 : half + 8, :]])
-    far_choice = (one_hot(got[0]), got[1])
-    order = []
-    for part in range(PARTS // 2):
-        order += [(0, part), (1, part + PARTS // 2)]
-    for side, part in order:
-        ring_copy(side, half, part, own.at[:, pl.ds(0, width)]).wait_recv()
-        block = ring[side, half - 1, part]
-        pick_rows([far_choice + (block,)], picked_far, arrived_far, half, part, PAD)
-    add_hop(half - 1)
-    far = lax.rem(z + half, nz)
+    drain_ring(half - 1, going_on)
+    drain_hop(half - 2)
+
+    def stacked_rows(level):
+        block = hidden[level].astype(f32)
+        pieces = [block[source * send : (source + 1) * send] for source in range(nx)]
+        gap = jnp.zeros((send, hidden.shape[2]), f32)
+        first = jnp.concatenate([p for piece in pieces for p in (piece, gap)], axis=0)
+        second = jnp.concatenate([p for piece in pieces for p in (gap, piece)], axis=0)
+        return [jnp.transpose(v).astype(bf16) for v in (first, second)]
+
+    def product(lhs, buffer):
+        rows = buffer.reshape(nx * 2 * send, width)
+        return jnp.dot(lhs, rows, preferred_element_type=f32)
+
+    before, after = pair_levels(half - 1)
+    lhs_sides = [stacked_rows(before), stacked_rows(after)]
+    lhs_far = stacked_rows(lax.rem(z + half, nz))
+    for side in range(2):
+        for step in range(1, nx):
+            origin = lax.rem(x + nx - step, nx)
+            x_copy(picked_near, arrived_near, half - 1, side, step, origin).wait_recv()
+    for side in range(2):
+        for step in range(nx):
+            direct_copy(0, side, step, lax.rem(x + nx - step, nx)).wait_recv()
+    for side in range(2):
+        for index, part in enumerate(kept[side]):
+            merged[:, part * width : (part + 1) * width] += product(
+                lhs_sides[side][index], arrived_near[side]
+            ) + product(lhs_sides[1 - side][index], direct_in[0, 1 - side])
+
     rank = q_rows.shape[0]
     ff = merged.shape[0]
     q_parts = thirds(q_rows[...])
@@ -281,9 +348,14 @@
                 piece, q_stacks[i][:, cols], (((1,), (1,)), ((), ())), preferred_element_type=f32
             )
 
-    accumulate(
-        arrived_far, picked_far, half, [far], PAD, [part for _, part in order], left_product
-    )
+    for side in range(2):
+        for step in range(nx):
+            direct_copy(1, side, step, lax.rem(x + nx - step, nx)).wait_recv()
+        for index, part in enumerate(kept[side]):
+            merged[:, part * width : (part + 1) * width] += product(
+                lhs_far[index], direct_in[1, side]
+            )
+            left_product(part)
     stacked = jnp.transpose(left_turned[0])
     left_local = (stacked[2 * rank : 3 * rank] + stacked[rank : 2 * rank]) + stacked[:rank]
 
@@ -338,10 +410,11 @@
     save_merged = pltpu.make_async_copy(merged, merged_hbm, local_sem.at[3])
     save_merged.start()
 
-    drain_ring(half, last)
-    drain_x(half - 2)
-    drain_x(half - 1, picked_own, arrived_own)
-    drain_x(half, picked_far, arrived_far)
+    drain_x(half - 1, picked_near, arrived_near, range(2))
+    for stage in range(2):
+        for side in range(2):
+            for step in range(nx):
+                direct_copy(stage, side, step).wait_send()
 
     end_sum(left_out, left_in, left_all, 0)
     left_sum = collect(left_all, 0)
@@ -392,10 +465,38 @@
             dp_copy(source.at[0], source, stage, step, replica).wait_send()
 
 
-def apply_kernel(merged, basis_stack, q_stack, q_new, new_error, q_next):
-    approx = jnp.dot(basis_stack[...], q_stack[...], preferred_element_type=f32)
-    new_error[...] = (merged[...] - approx).astype(bf16)
-    q_next[...] = q_new[...]
+def apply_kernel(
+    merged_hbm, basis_hbm, stack_hbm, q_hbm, error_hbm, next_hbm,
+    merged, basis_stack, q_stack, new_error, load_sem, small_sem, store_sem,
+):
+    rows = merged.shape[1]
+    small = [
+        pltpu.make_async_copy(basis_hbm, basis_stack, small_sem.at[0]),
+        pltpu.make_async_copy(stack_hbm, q_stack, small_sem.at[1]),
+        pltpu.make_async_copy(q_hbm, next_hbm, small_sem.at[2]),
+    ]
+    loads = [
+        pltpu.make_async_copy(merged_hbm.at[pl.ds(i * rows, rows)], merged.at[i], load_sem.at[i])
+        for i in range(STEPS)
+    ]
+    stores = [
+        pltpu.make_async_copy(new_error.at[i], error_hbm.at[pl.ds(i * rows, rows)], store_sem.at[i])
+        for i in range(STEPS)
+    ]
+    for copy in small + loads:
+        copy.start()
+    small[0].wait()
+    small[1].wait()
+    for i in range(STEPS):
+        loads[i].wait()
+        approx = jnp.dot(
+            basis_stack[i * rows : (i + 1) * rows], q_stack[...], preferred_element_type=f32
+        )
+        new_error[i] = (merged[i] - approx).astype(bf16)
+        stores[i].start()
+    small[2].wait()
+    for copy in stores:
+        copy.wait()
 
 
 def shards(cotangent, route_weights, expert_ids, slot_index, hidden, carried_error, q_factor):
@@ -427,13 +528,15 @@
             pltpu.VMEM((ff, model_dim), f32),
             pltpu.VMEM((3, ff, model_dim), bf16),
             pltpu.VMEM((tokens, model_dim), bf16),
-            pltpu.VMEM((2, half, PARTS, tokens, width), bf16),
-            pltpu.VMEM((2, half + 1, 16, 128), f32),
+            pltpu.VMEM((2, half - 1, PARTS, tokens, width), bf16),
+            pltpu.VMEM((2, half, 16, 128), f32),
             pltpu.VMEM((32, 128), f32),
-            pltpu.VMEM((half - 1, PARTS, nx, 2 * send, width), bf16),
-            pltpu.VMEM((half - 1, PARTS, nx, 2 * send, width), bf16),
+            pltpu.VMEM((half - 2, PARTS, nx, 2 * send, width), bf16),
+            pltpu.VMEM((half - 2, PARTS, nx, 2 * send, width), bf16),
         ]
-        + [pltpu.VMEM((PARTS, nx, PAD, width), bf16)] * 4
+        + [pltpu.VMEM((PARTS, nx, PAD, width), bf16)] * 2
+        + [pltpu.VMEM((2, nx, 2 * send, width), bf16)] * 2
+        + [pltpu.VMEM((2, 2, nx, 2 * send, width), bf16)] * 2
         + [
             pltpu.VMEM((nz, nx * send, ff), bf16),
             pltpu.VMEM((ff, model_dim), bf16),
@@ -442,12 +545,14 @@
         + [pltpu.VMEM((replicas, share, 1, model_dim), f32)] * 3
         + [
             dma((4,)),
-            dma((2, half, PARTS)),
-            dma((2, half, PARTS)),
-            dma((2, half)),
-            dma((2, half)),
-            dma((half + 1, PARTS, nx - 1)),
-            dma((half + 1, PARTS, nx - 1)),
+            dma((2, half - 1, PARTS)),
+            dma((2, half - 1, PARTS)),
+            dma((2, half - 1)),
+            dma((2, half - 1)),
+            dma((half, PARTS, nx - 1)),
+            dma((half, PARTS, nx - 1)),
+            dma((2, 2, nx)),
+            dma((2, 2, nx)),
             dma((4, max(replicas - 1, 1))),
             dma((4, max(replicas - 1, 1))),
         ],
@@ -467,21 +572,21 @@
     rows = ff // STEPS
     new_error, q_next = pl.pallas_call(
         apply_kernel,
-        grid=(STEPS,),
         out_shape=(
             jax.ShapeDtypeStruct((ff, model_dim), bf16),
             jax.ShapeDtypeStruct((rank, model_dim), f32),
         ),
-        in_specs=[
-            pl.BlockSpec((rows, model_dim), lambda i: (i, 0)),
-            pl.BlockSpec((rows, 128), lambda i: (i, 0)),
-            pl.BlockSpec((128, model_dim), lambda i: (0, 0)),
-            pl.BlockSpec((rank, model_dim), lambda i: (0, 0)),
+        in_specs=[hbm] * 4,
+        out_specs=(hbm, hbm),
+        scratch_shapes=[
+            pltpu.VMEM((STEPS, rows, model_dim), f32),
+            pltpu.VMEM((ff, 128), bf16),
+            pltpu.VMEM((128, model_dim), bf16),
+            pltpu.VMEM((STEPS, rows, model_dim), bf16),
+            dma((STEPS,)),
+            dma((3,)),
+            dma((STEPS,)),
         ],
-        out_specs=(
-            pl.BlockSpec((rows, model_dim), lambda i: (i, 0)),
-            pl.BlockSpec((rank, model_dim), lambda i: (0, 0)),
-        ),
         compiler_params=pltpu.CompilerParams(vmem_limit_bytes=VMEM_BYTES),
         name="apply_factors",
     )(merged, basis_stack, q_stack, q_new)

time: 128 us -> 123 us (0.961)
  Pallas kernels: 127 us -> 123 us
    pallas_call x1, Pallas kernels: 123 us -> 119 us  [shards(): pl.pallas_call(functools.partial(kernel, nz, nx, send, replicas), out_sha...]
where the time goes in v4:
time: 123 us
  Pallas kernels  123 us (100%)
    pallas_call x1, Pallas kernels, shards(): pl.pallas_call(functools.partial(kernel, nz, nx, send, replicas), out_sha...  119 us
    pallas_call x1, Pallas kernels, shards(): pl.pallas_call(apply_kernel, out_shape=(jax.ShapeDtypeStruct((ff, model_d...  3.19 us

profile of v4, /device:TPU:1, one launch (start us, length us, event | category | flops | bytes accessed | tf_op | source)
XLA Modules:
  0.0 123.2 jit_solution(17315882926111571094)
XLA Ops:
  0.6 119.4 %route_and_factor.1 = (f32[384,1024]{1,0:T(8,128)}, bf16[384,128]{1,0:T(8,128)(2,1)}, bf16[128,1024]{1,0:T(8,128)(2,1)}, f32[16,1024]{1,0:T(8,128)}) custom-call(bf16[192,1024]{1,0:T(8,128)(2,1)} %bitcast.17, f32[8,192]{1,0:T(8,128)} %bitcast.19, s32[8,192]{1,0:T(8,128)} %bitcast.20, s32[8,192]{1,0:T(8,128)} %bitcast.21, bf16[16,96,384]{2,1,0:T(8,128)(2,1)} %bitcast.15, ...), custom_call_target="tpu_custom_call" | custom-call | tf_op jit(solution)/shard_map/route_and_factor/pallas_call | solution.py:517
  120.0 3.2 %apply_factors.1 = (bf16[384,1024]{1,0:T(8,128)(2,1)}, f32[16,1024]{1,0:T(8,128)}) custom-call(f32[384,1024]{1,0:T(8,128)} %get-tuple-element.8.merged_hbm, bf16[384,128]{1,0:T(8,128)(2,1)} %get-tuple-element.9.basis_hbm, bf16[128,1024]{1,0:T(8,128)(2,1)} %get-tuple-element.10.stack_hbm, f32[16,1024]{1,0:T(8,128)} %get-tuple-element.11.q_hbm), custom_call_target="tpu_custom_call" | custom-call | tf_op jit(solution)/shard_map/apply_factors/pallas_call | solution.py:573

commit v5 on v4

--- a/solution.py
+++ b/solution.py
@@ -25,14 +25,19 @@
     return first, second, value - first - second
 
 
+def halves(value):
+    first = value.astype(bf16).astype(f32)
+    return first, value - first
+
+
 def kernel(
     nz, nx, send, replicas,
-    cot, weights, ids, slots, hidden_hbm, error_hbm, q_rows,
-    merged_hbm, basis_stack, q_stack, q_next,
-    merged, splits, own, ring, meta, own_meta, picked, arrived, picked_own, arrived_own, picked_near, arrived_near, direct_out, direct_in,
+    cot, weights_hbm, ids_hbm, slots_hbm, hidden_hbm, error_hbm, q_hbm,
+    merged_hbm, basis_hbm, q_next,
+    weights, ids, slots, q_rows, basis_stack, merged, splits, own, ring, meta, own_meta, picked, arrived, picked_own, arrived_own, picked_near, arrived_near, direct_out, direct_in,
     hidden, error,
     left_out, left_in, left_all, right_out, right_in, right_all,
-    local_sem, ring_send, ring_recv, meta_send, meta_recv, x_send, x_recv,
+    local_sem, small_sem, ring_send, ring_recv, meta_send, meta_recv, x_send, x_recv,
     direct_send, direct_recv, dp_send, dp_recv,
 ):
     half = nz // 2
@@ -50,6 +55,14 @@
     load_error = pltpu.make_async_copy(error_hbm, error, local_sem.at[1])
     load_own = pltpu.make_async_copy(cot, own, local_sem.at[2])
     load_own.start()
+    load_small = [
+        pltpu.make_async_copy(source, target, small_sem.at[i])
+        for i, (source, target) in enumerate(
+            ((ids_hbm, ids), (slots_hbm, slots), (weights_hbm, weights), (q_hbm, q_rows))
+        )
+    ]
+    for load in load_small:
+        load.start()
 
     barrier = pltpu.get_barrier_semaphore()
     levels = (lax.rem(z + 1, nz), lax.rem(z + nz - 1, nz))
@@ -120,6 +133,8 @@
     load_hidden.start()
     load_error.start()
 
+    for load in load_small:
+        load.wait()
     routes = ids.shape[0]
     spot = lax.broadcasted_iota(jnp.int32, (128, tokens), 0)
     token = lax.broadcasted_iota(jnp.int32, (128, tokens), 1).astype(f32)
@@ -190,9 +205,8 @@
             pieces += [b[source * send : (source + 1) * send] for b in blocks] + filler
         return jnp.transpose(jnp.concatenate(pieces, axis=0)).astype(bf16)
 
-    def accumulate(land, pick, group, levels, rows):
-        turned = hidden_rows(levels, rows)
-        for part in range(PARTS):
+    def accumulate(land, pick, group, turned, rows, parts):
+        for part in parts:
             for step in range(1, nx):
                 x_copy(pick, land, group, part, step, lax.rem(x + nx - step, nx)).wait_recv()
             block = land[part].reshape(nx * rows, width)
@@ -203,7 +217,7 @@
     def pair_levels(hop):
         return [lax.rem(z - hop + nz, nz), lax.rem(z + hop, nz)]
 
-    def step_hop(hop, forward):
+    def step_hop(hop, forward, add):
         choices = None
         for slot, parts in enumerate(order):
             for side in range(2):
@@ -215,7 +229,9 @@
                     meta_copy(side, hop).wait_recv()
                     meta_copy(side, hop + 1).start()
                 choices = choices_of(hop, hop)
-            if slot >= turn:
+            if slot < turn:
+                add(parts)
+            else:
                 for part in parts:
                     blocks = [choices[s] + (ring[s, hop - 1, part],) for s in range(2)]
                     pick_rows(blocks, picked.at[hop - 1, part], 2 * send)
@@ -230,8 +246,14 @@
             for step in range(nx):
                 direct_copy(stage, side, step).start()
 
-    def add_hop(hop):
-        accumulate(arrived.at[hop - 1], picked.at[hop - 1], hop - 1, pair_levels(hop), 2 * send)
+    def adder(hop):
+        turned = hidden_rows(pair_levels(hop), 2 * send)
+        group = hop - 1
+
+        def add(parts):
+            accumulate(arrived.at[group], picked.at[group], group, turned, 2 * send, parts)
+
+        return add
 
     everything = lambda side, part: True
     going_on = lambda side, part: part in kept[side]
@@ -262,8 +284,11 @@
     merged[...] = error[...].astype(f32)
     load_hidden.wait()
 
-    step_hop(1, everything)
-    accumulate(arrived_own, picked_own, half - 2, [z], PAD)
+    turned_own = hidden_rows([z], PAD)
+    add_own = lambda parts: accumulate(
+        arrived_own, picked_own, half - 2, turned_own, PAD, parts
+    )
+    step_hop(1, everything, add_own)
     for part in range(PARTS):
         for side in range(2):
             own_copy(side, part).wait_send()
@@ -272,16 +297,14 @@
     drain_x(half - 2, picked_own, arrived_own)
 
     def body(hop, carry):
-        step_hop(hop, everything)
-        add_hop(hop - 1)
+        step_hop(hop, everything, adder(hop - 1))
         drain_ring(hop)
         drain_hop(hop - 1)
         return carry
 
     lax.fori_loop(2, half - 2, body, 0)
-    step_hop(half - 2, going_on)
+    step_hop(half - 2, going_on, adder(half - 3))
     send_direct(0, half - 2)
-    add_hop(half - 3)
     drain_ring(half - 2)
     drain_hop(half - 3)
 
@@ -296,7 +319,7 @@
         blocks = [choices[side] + (ring[side, half - 2, part],) for part in kept[side]]
         pick_rows(blocks, picked_near.at[side], 2 * send)
         pass_rows(picked_near, arrived_near, half - 1, side)
-    add_hop(half - 2)
+    adder(half - 2)(range(PARTS))
     drain_ring(half - 1, going_on)
     drain_hop(half - 2)
 
@@ -330,18 +353,18 @@
 
     rank = q_rows.shape[0]
     ff = merged.shape[0]
-    q_parts = thirds(q_rows[...])
-    blank = jnp.zeros((128 - 3 * rank, model_dim), f32)
+    q_parts = halves(q_rows[...])
+    blank = jnp.zeros((128 - 2 * rank, model_dim), f32)
     none = jnp.zeros((rank, model_dim), f32)
     q_stacks = [
-        jnp.concatenate(list(q_parts[: 3 - i]) + [none] * i + [blank], axis=0).astype(bf16)
-        for i in range(3)
+        jnp.concatenate(list(q_parts[: 2 - i]) + [none] * i + [blank], axis=0).astype(bf16)
+        for i in range(2)
     ]
     left_turned = [jnp.zeros((ff, 128), f32)]
 
     def left_product(part):
         cols = slice(part * width, (part + 1) * width)
-        for i, piece in enumerate(thirds(merged[:, cols])):
+        for i, piece in enumerate(halves(merged[:, cols])):
             piece = piece.astype(bf16)
             splits[i, :, cols] = piece
             left_turned[0] += lax.dot_general(
@@ -357,7 +380,7 @@
             )
             left_product(part)
     stacked = jnp.transpose(left_turned[0])
-    left_local = (stacked[2 * rank : 3 * rank] + stacked[rank : 2 * rank]) + stacked[:rank]
+    left_local = stacked[rank : 2 * rank] + stacked[:rank]
 
     share = rank // replicas
 
@@ -419,13 +442,13 @@
     end_sum(left_out, left_in, left_all, 0)
     left_sum = collect(left_all, 0)
 
-    left_parts = thirds(left_sum)
+    left_parts = halves(left_sum)
     left_stack = jnp.concatenate(left_parts, axis=0).astype(bf16)
     right_local = None
-    for i in (2, 1, 0):
-        product = jnp.dot(left_stack[: (3 - i) * rank], splits[i], preferred_element_type=f32)
-        for j in range(2 - i, -1, -1):
-            term = product[j * rank : (j + 1) * rank]
+    for i in (1, 0):
+        terms = jnp.dot(left_stack[: (2 - i) * rank], splits[i], preferred_element_type=f32)
+        for j in range(1 - i, -1, -1):
+            term = terms[j * rank : (j + 1) * rank]
             right_local = term if right_local is None else right_local + term
     begin_sum(right_local, right_out, right_in, 2)
 
@@ -444,21 +467,30 @@
         ratio = jnp.where(row_of > k, gram[:, k : k + 1] / pivot, 0.0)
         gram, inverse = gram - ratio * gram[k : k + 1], inverse - ratio * inverse[k : k + 1]
     inverse = inverse / jnp.sqrt(pivots)
-    basis = jnp.dot(inverse, left_sum, precision=highest, preferred_element_type=f32)
-    b1, b2, b3 = thirds(basis)
-    blank = jnp.zeros((128 - 6 * rank, ff), f32)
+    i1, i2 = halves(inverse)
+    inverse_stack = jnp.concatenate([i1, i1, i2], axis=1).astype(bf16)
+
+    end_sum(right_out, right_in, right_all, 2)
+    l1, l2 = left_parts
+    basis = jnp.dot(
+        inverse_stack, jnp.concatenate([l1, l2, l1], axis=0).astype(bf16),
+        preferred_element_type=f32,
+    )
+    b1, b2 = halves(basis)
+    blank = jnp.zeros((128 - 3 * rank, ff), f32)
     basis_stack[...] = jnp.transpose(
-        jnp.concatenate([b1, b1, b1, b2, b2, b3, blank], axis=0)
+        jnp.concatenate([b1, b1, b2, blank], axis=0)
     ).astype(bf16)
-
-    end_sum(right_out, right_in, right_all, 2)
+    save_basis = pltpu.make_async_copy(basis_stack, basis_hbm, local_sem.at[4])
+    save_basis.start()
     right_sum = collect(right_all, 2)
-    q_new = jnp.dot(inverse, right_sum, precision=highest, preferred_element_type=f32)
-    q_next[...] = q_new
-    p1, p2, p3 = thirds(q_new)
-    blank = jnp.zeros((128 - 6 * rank, model_dim), f32)
-    q_stack[...] = jnp.concatenate([p1, p2, p3, p1, p2, p1, blank], axis=0).astype(bf16)
+    r1, r2 = halves(right_sum)
+    q_next[...] = jnp.dot(
+        inverse_stack, jnp.concatenate([r1, r2, r1], axis=0).astype(bf16),
+        preferred_element_type=f32,
+    )
     save_merged.wait()
+    save_basis.wait()
     for stage, source in enumerate((left_out, left_all, right_out, right_all)):
         @pl.loop(1, replicas)
         def _(step):
@@ -466,14 +498,13 @@
 
 
 def apply_kernel(
-    merged_hbm, basis_hbm, stack_hbm, q_hbm, error_hbm, next_hbm,
-    merged, basis_stack, q_stack, new_error, load_sem, small_sem, store_sem,
+    merged_hbm, basis_hbm, q_hbm, error_hbm, next_hbm,
+    merged, basis_stack, q_new, new_error, load_sem, small_sem, store_sem,
 ):
     rows = merged.shape[1]
     small = [
-        pltpu.make_async_copy(basis_hbm, basis_stack, small_sem.at[0]),
-        pltpu.make_async_copy(stack_hbm, q_stack, small_sem.at[1]),
-        pltpu.make_async_copy(q_hbm, next_hbm, small_sem.at[2]),
+        pltpu.make_async_copy(q_hbm, q_new, small_sem.at[0]),
+        pltpu.make_async_copy(basis_hbm, basis_stack, small_sem.at[1]),
     ]
     loads = [
         pltpu.make_async_copy(merged_hbm.at[pl.ds(i * rows, rows)], merged.at[i], load_sem.at[i])
@@ -483,18 +514,23 @@
         pltpu.make_async_copy(new_error.at[i], error_hbm.at[pl.ds(i * rows, rows)], store_sem.at[i])
         for i in range(STEPS)
     ]
+    save_next = pltpu.make_async_copy(q_new, next_hbm, small_sem.at[2])
     for copy in small + loads:
         copy.start()
     small[0].wait()
+    save_next.start()
+    q1, q2 = halves(q_new[...])
+    blank = jnp.zeros((128 - 3 * q1.shape[0], q1.shape[1]), f32)
+    q_stack = jnp.concatenate([q1, q2, q1, blank], axis=0).astype(bf16)
     small[1].wait()
     for i in range(STEPS):
         loads[i].wait()
         approx = jnp.dot(
-            basis_stack[i * rows : (i + 1) * rows], q_stack[...], preferred_element_type=f32
+            basis_stack[i * rows : (i + 1) * rows], q_stack, preferred_element_type=f32
         )
         new_error[i] = (merged[i] - approx).astype(bf16)
         stores[i].start()
-    small[2].wait()
+    save_next.wait()
     for copy in stores:
         copy.wait()
 
@@ -514,19 +550,23 @@
     dma = pltpu.SemaphoreType.DMA
     rank = q_factor.shape[1]
     share = rank // replicas
-    merged, basis_stack, q_stack, q_new = pl.pallas_call(
+    merged, basis_stack, q_new = pl.pallas_call(
         functools.partial(kernel, nz, nx, send, replicas),
         out_shape=(
             jax.ShapeDtypeStruct((ff, model_dim), f32),
             jax.ShapeDtypeStruct((ff, 128), bf16),
-            jax.ShapeDtypeStruct((128, model_dim), bf16),
             jax.ShapeDtypeStruct((rank, model_dim), f32),
         ),
-        in_specs=[hbm] + [vmem] * 3 + [hbm] * 2 + [vmem],
-        out_specs=(hbm, vmem, vmem, vmem),
+        in_specs=[hbm] * 7,
+        out_specs=(hbm, hbm, vmem),
         scratch_shapes=[
+            pltpu.VMEM(route_weights.shape[1:][::-1], f32),
+            pltpu.VMEM(expert_ids.shape[1:][::-1], jnp.int32),
+            pltpu.VMEM(slot_index.shape[1:][::-1], jnp.int32),
+            pltpu.VMEM((rank, model_dim), f32),
+            pltpu.VMEM((ff, 128), bf16),
             pltpu.VMEM((ff, model_dim), f32),
-            pltpu.VMEM((3, ff, model_dim), bf16),
+            pltpu.VMEM((2, ff, model_dim), bf16),
             pltpu.VMEM((tokens, model_dim), bf16),
             pltpu.VMEM((2, half - 1, PARTS, tokens, width), bf16),
             pltpu.VMEM((2, half, 16, 128), f32),
@@ -544,6 +584,7 @@
         + [pltpu.VMEM((replicas, share, 1, ff), f32)] * 3
         + [pltpu.VMEM((replicas, share, 1, model_dim), f32)] * 3
         + [
+            dma((5,)),
             dma((4,)),
             dma((2, half - 1, PARTS)),
             dma((2, half - 1, PARTS)),
@@ -576,12 +617,12 @@
             jax.ShapeDtypeStruct((ff, model_dim), bf16),
             jax.ShapeDtypeStruct((rank, model_dim), f32),
         ),
-        in_specs=[hbm] * 4,
+        in_specs=[hbm] * 3,
         out_specs=(hbm, hbm),
         scratch_shapes=[
             pltpu.VMEM((STEPS, rows, model_dim), f32),
             pltpu.VMEM((ff, 128), bf16),
-            pltpu.VMEM((128, model_dim), bf16),
+            pltpu.VMEM((rank, model_dim), f32),
             pltpu.VMEM((STEPS, rows, model_dim), bf16),
             dma((STEPS,)),
             dma((3,)),
@@ -589,7 +630,7 @@
         ],
         compiler_params=pltpu.CompilerParams(vmem_limit_bytes=VMEM_BYTES),
         name="apply_factors",
-    )(merged, basis_stack, q_stack, q_new)
+    )(merged, basis_stack, q_new)
     return (new_error[None, None], q_next[None])
 
 

time: 123 us -> 122 us (level)
  Pallas kernels: 123 us -> 121 us
    pallas_call x1, Pallas kernels: 119 us -> 118 us  [shards(): pl.pallas_call(functools.partial(kernel, nz, nx, send, replicas), out_sha...]
where the time goes in v5:
time: 122 us; the launch traced here: 121 us
  Pallas kernels  121 us (99%)
    pallas_call x1, Pallas kernels, shards(): pl.pallas_call(functools.partial(kernel, nz, nx, send, replicas), out_sha...  118 us
    pallas_call x1, Pallas kernels, shards(): pl.pallas_call(apply_kernel, out_shape=(jax.ShapeDtypeStruct((ff, model_d...  2.78 us

profile of v5, /device:TPU:1, one launch (start us, length us, event | category | flops | bytes accessed | tf_op | source)
XLA Modules:
  0.0 121.5 jit_solution(12830434388876925160)
XLA Ops:
  0.6 118.0 %route_and_factor.1 = (f32[384,1024]{1,0:T(8,128)}, bf16[384,128]{1,0:T(8,128)(2,1)}, f32[16,1024]{1,0:T(8,128)}) custom-call(bf16[192,1024]{1,0:T(8,128)(2,1)} %bitcast.17, f32[8,192]{1,0:T(8,128)} %bitcast.19, s32[8,192]{1,0:T(8,128)} %bitcast.20, s32[8,192]{1,0:T(8,128)} %bitcast.21, bf16[16,96,384]{2,1,0:T(8,128)(2,1)} %bitcast.15, ...), custom_call_target="tpu_custom_call" | custom-call | tf_op jit(solution)/shard_map/route_and_factor/pallas_call | solution.py:553
  118.7 2.8 %apply_factors.1 = (bf16[384,1024]{1,0:T(8,128)(2,1)}, f32[16,1024]{1,0:T(8,128)}) custom-call(f32[384,1024]{1,0:T(8,128)} %get-tuple-element.7.merged_hbm, bf16[384,128]{1,0:T(8,128)(2,1)} %get-tuple-element.8.basis_hbm, f32[16,1024]{1,0:T(8,128)} %get-tuple-element.9.q_hbm), custom_call_target="tpu_custom_call" | custom-call | tf_op jit(solution)/shard_map/apply_factors/pallas_call | solution.py:614

commit v6 on v5

--- a/solution.py
+++ b/solution.py
@@ -71,7 +71,7 @@
     for partner in partners:
         pl.semaphore_signal(barrier, inc=1, device_id={"expert": partner}, device_id_type=MESH)
     replica = lax.axis_index("dp")
-    for step in range(1, replicas):
+    for step in sorted(range(1, replicas), key=lambda v: -min(v, replicas - v)):
         partner = lax.rem(replica + step, replicas)
         pl.semaphore_signal(barrier, inc=1, device_id={"dp": partner}, device_id_type=MESH)
     pl.semaphore_wait(barrier, len(partners) + replicas - 1)
@@ -243,7 +243,7 @@
             parts = kept[side] if stage else kept[1 - side]
             blocks = [choices[side] + (ring[side, hop - 1, part],) for part in parts]
             pick_rows(blocks, direct_out.at[stage, side], 2 * send)
-            for step in range(nx):
+            for step in sorted(range(nx), key=lambda v: -min(v, nx - v)):
                 direct_copy(stage, side, step).start()
 
     def adder(hop):
@@ -384,6 +384,9 @@
 
     share = rank // replicas
 
+    def far_first(turn):
+        return replicas // 2 + (2 * lax.rem(turn, 2) - 1) * lax.div(turn, 2)
+
     def dp_copy(source, target, stage, step, origin):
         return pltpu.make_async_remote_copy(
             src_ref=source,
@@ -398,7 +401,8 @@
         for row in range(rank):
             out[row // share, row % share] = value[row : row + 1]
         @pl.loop(1, replicas)
-        def _(step):
+        def _(turn):
+            step = far_first(turn)
             target = lax.rem(replica + step, replicas)
             dp_copy(out.at[target], into, stage, step, replica).start()
 
@@ -416,8 +420,8 @@
         gathered[replica] = total * (1.0 / replicas)
 
         @pl.loop(1, replicas)
-        def _(step):
-            dp_copy(gathered.at[replica], gathered, stage + 1, step, replica).start()
+        def _(turn):
+            dp_copy(gathered.at[replica], gathered, stage + 1, far_first(turn), replica).start()
 
     def collect(gathered, stage):
         @pl.loop(1, replicas)

time: 122 us -> 120 us (0.984)
  Pallas kernels: 121 us -> 119 us
    pallas_call x1, Pallas kernels: 118 us -> 116 us  [shards(): pl.pallas_call(functools.partial(kernel, nz, nx, send, replicas), out_sha...]
where the time goes in v6:
time: 120 us; the launch traced here: 119 us
  Pallas kernels  119 us (99%)
    pallas_call x1, Pallas kernels, shards(): pl.pallas_call(functools.partial(kernel, nz, nx, send, replicas), out_sha...  116 us
    pallas_call x1, Pallas kernels, shards(): pl.pallas_call(apply_kernel, out_shape=(jax.ShapeDtypeStruct((ff, model_d...  2.78 us

profile of v6, /device:TPU:1, one launch (start us, length us, event | category | flops | bytes accessed | tf_op | source)
XLA Modules:
  0.0 119.4 jit_solution(18265414985788636965)
XLA Ops:
  0.6 116.0 %route_and_factor.1 = (f32[384,1024]{1,0:T(8,128)}, bf16[384,128]{1,0:T(8,128)(2,1)}, f32[16,1024]{1,0:T(8,128)}) custom-call(bf16[192,1024]{1,0:T(8,128)(2,1)} %bitcast.17, f32[8,192]{1,0:T(8,128)} %bitcast.19, s32[8,192]{1,0:T(8,128)} %bitcast.20, s32[8,192]{1,0:T(8,128)} %bitcast.21, bf16[16,96,384]{2,1,0:T(8,128)(2,1)} %bitcast.15, ...), custom_call_target="tpu_custom_call" | custom-call | tf_op jit(solution)/shard_map/route_and_factor/pallas_call | solution.py:557
  116.6 2.8 %apply_factors.1 = (bf16[384,1024]{1,0:T(8,128)(2,1)}, f32[16,1024]{1,0:T(8,128)}) custom-call(f32[384,1024]{1,0:T(8,128)} %get-tuple-element.7.merged_hbm, bf16[384,128]{1,0:T(8,128)(2,1)} %get-tuple-element.8.basis_hbm, f32[16,1024]{1,0:T(8,128)} %get-tuple-element.9.q_hbm), custom_call_target="tpu_custom_call" | custom-call | tf_op jit(solution)/shard_map/apply_factors/pallas_call | solution.py:618
